TPU v7x, 32 devices: a whole 2x2x4 slice. The times are simulated.
32 devices in a mesh: quad: 4 (over z), slab: 8 (over y, x, core).
Axes of the slice: x: 2, y: 2, z: 4, core: 2. Of those that a mesh axis runs over, the one named last changes fastest.
Arguments:
- factors: bfloat16 [4, 8, 2, 512, 512], P('quad', 'slab'), may hold values from -0.1875 to 0.1875
- onsite: float32 [8, 512, 512], P('slab'), may hold values from -0.25 to 0.25, as said below
- coupling: float32 [8, 128, 128], P('slab'), may hold values from -1 to 1
- vectors: bfloat16 [8, 512, 128], P('slab'), may hold values from -1.5 to 1.5
- quad_weight: float32 [4, 2], P('quad'), may hold values from -0.6 to 0.6
Outputs:
- subspace: float32 [8, 512, 128], P('slab', 'quad')
- correlation: float32 [128, 128], replicated
- projected: float32 [128, 128], replicated
Inputs may be any that keep to these rules, and one draw needn't show every extreme that they name: `onsite`: each diagonal block is symmetric, and its largest entry magnitude is exactly 8 / sqrt(1024).
All inputs are finite; a program needn't handle non-finite values.
Results may differ from a plain program's by a relative error of at most 0.0003.
Values sent between devices are 32-bit elements; how exact they have to be, the bound alone decides.
A program may use at most 64 MiB of HBM per device.

v0:
```python
import jax
import jax.numpy as jnp
from jax import lax
from jax.sharding import PartitionSpec as P

precise = lax.Precision.HIGHEST


def prefix(x, axis, combine, identity, reverse):
    count, mine = (lax.axis_size(axis), lax.axis_index(axis))
    everything = jax.tree.map(lambda part: lax.all_gather(part, axis), x)
    start = jax.tree.map(
        lambda part, zero: jnp.broadcast_to(jnp.asarray(zero, part.dtype), part.shape), x, identity
    )

    def step(k, before):
        at = count - 1 - k if reverse else k
        reached = at > mine if reverse else at < mine
        new = combine(before, jax.tree.map(lambda part: part[at], everything))
        return jax.tree.map(lambda a, b: jnp.where(reached, a, b), new, before)

    return lax.fori_loop(0, count, step, start)


def shifted(block, axis, distance):
    devices = range(lax.axis_size(axis))
    route = [(i - distance, i) for i in devices if i - distance in devices]
    return lax.ppermute(block, axis, route)


def complex_times(left_cols, right_cols):
    real_part = jnp.dot(
        left_cols[0], right_cols[0], precision=precise, preferred_element_type=jnp.float32
    ) - jnp.dot(left_cols[1], right_cols[1], precision=precise, preferred_element_type=jnp.float32)
    imag_part = jnp.dot(
        left_cols[0], right_cols[1], precision=precise, preferred_element_type=jnp.float32
    ) + jnp.dot(left_cols[1], right_cols[0], precision=precise, preferred_element_type=jnp.float32)
    return jnp.stack([real_part, imag_part])


def real_times(real_left, right_cols):
    return jnp.stack(
        [
            jnp.dot(
                real_left, right_cols[0], precision=precise, preferred_element_type=jnp.float32
            ),
            jnp.dot(
                real_left, right_cols[1], precision=precise, preferred_element_type=jnp.float32
            ),
        ]
    )


def times_real(left_cols, real_right):
    return jnp.stack(
        [
            jnp.dot(
                left_cols[0], real_right, precision=precise, preferred_element_type=jnp.float32
            ),
            jnp.dot(
                left_cols[1], real_right, precision=precise, preferred_element_type=jnp.float32
            ),
        ]
    )


def compose(earlier, later):
    return (complex_times(later[0], earlier[0]), complex_times(later[0], earlier[1]) + later[1])


def half_plus_upper(field_rows, next_rows, onsite, coupling):
    orbitals = field_rows.shape[1]
    plane_rows = coupling.shape[1]
    half_diag = 0.5 * jnp.dot(
        onsite[0], field_rows[0], precision=precise, preferred_element_type=jnp.float32
    )
    upper_part = jnp.dot(
        coupling[0], next_rows, precision=precise, preferred_element_type=jnp.float32
    )
    pieces = [
        jnp.concatenate(
            [half_diag[: orbitals - plane_rows], half_diag[orbitals - plane_rows :] + upper_part],
            axis=0,
        )
    ]
    return jnp.stack(pieces)


def tile_sums(field_rows, weighted):
    columns = field_rows.shape[2]
    flattened = field_rows.reshape(-1, columns)
    gram_part = lax.dot_general(
        flattened,
        flattened,
        (((0,), (0,)), ((), ())),
        precision=precise,
        preferred_element_type=jnp.float32,
    )
    weighted_part = lax.dot_general(
        flattened,
        weighted.reshape(-1, columns),
        (((0,), (0,)), ((), ())),
        precision=precise,
        preferred_element_type=jnp.float32,
    )
    return (gram_part, weighted_part)


def per_device(factors, onsite, coupling, vectors, quad_weight):
    slabs_here = factors.shape[1]
    orbitals = factors.shape[3]
    columns = vectors.shape[2]
    plane_rows = coupling.shape[1]
    unit_matrix = jnp.eye(plane_rows, dtype=jnp.float32)
    identity_pair = (
        jnp.stack([unit_matrix, jnp.zeros_like(unit_matrix)]),
        jnp.zeros((2, plane_rows, columns), jnp.float32),
    )
    slab_index = 0
    factor_block = factors[0, slab_index]
    sources = [
        jnp.dot(
            factor_block.reshape(2 * orbitals, orbitals),
            vectors[slab_index],
            preferred_element_type=jnp.float32,
        ).reshape(2, orbitals, columns)
    ]
    left_cols = [factor_block[:, :, :plane_rows].astype(jnp.float32)]
    right_cols = [factor_block[:, :, orbitals - plane_rows :].astype(jnp.float32)]
    forward_map = identity_pair
    slab_index = 0
    link_t = coupling[slab_index].T
    step_map = (
        real_times(link_t, left_cols[slab_index][:, orbitals - plane_rows :]),
        real_times(link_t, sources[slab_index][:, orbitals - plane_rows :]),
    )
    forward_map = compose(forward_map, step_map)
    incoming = prefix(forward_map, "slab", compose, identity_pair, False)[1]
    slab_index = 0
    solved = sources[slab_index] + complex_times(left_cols[slab_index], incoming)
    partial_rows = [solved]
    backward_map = identity_pair
    for slab_index in reversed(range(slabs_here)):
        step_map = (
            times_real(right_cols[slab_index][:, :plane_rows], coupling[slab_index]),
            partial_rows[slab_index][:, :plane_rows],
        )
        backward_map = compose(backward_map, step_map)
    incoming = prefix(backward_map, "slab", compose, identity_pair, True)[1]
    weight = quad_weight[0]
    filtered = []
    for slab_index in reversed(range(slabs_here)):
        result = partial_rows[slab_index] + complex_times(
            right_cols[slab_index], real_times(coupling[slab_index], incoming)
        )
        incoming = result[:, :plane_rows]
        filtered.append(weight[0] * result[0] - weight[1] * result[1])
    summed = jnp.stack(filtered[::-1])
    rows_all = slabs_here * orbitals * lax.axis_size("slab")
    whole = lax.psum(summed, "quad")
    next_rows = shifted(whole[0, :plane_rows], "slab", -1)
    weighted = half_plus_upper(whole, next_rows, onsite, coupling)
    gram_part, weighted_part = tile_sums(whole, weighted)
    gram_total, weighted_total = lax.psum((gram_part, weighted_part), "slab")
    share_rows = orbitals // lax.axis_size("quad")
    subspace = lax.dynamic_slice_in_dim(whole, lax.axis_index("quad") * share_rows, share_rows, 1)
    correlation = gram_total / rows_all
    projected = (weighted_total + weighted_total.T) / rows_all
    return (subspace, correlation, projected)


def solution(mesh):
    placed = (
        P("quad", "slab", None, None, None),
        P("slab", None, None),
        P("slab", None, None),
        P("slab", None, None),
        P("quad", None),
    )
    return jax.shard_map(
        per_device,
        mesh=mesh,
        in_specs=placed,
        out_specs=(P("slab", "quad", None), P(), P()),
        check_vma=False,
    )
```

profile of v0, /device:TPU:0, one launch (start us, length us, event | category | flops | bytes accessed | tf_op | source)
XLA Modules:
  0.0 283.2 jit_solution(3353942365164717578)
XLA Ops:
  7.2 1.2 fusion.64
  9.5 1.7 fusion.38
  15.9 23.3 %all-gather.8.cloned.1.call-done = f32[8,2,128,128]{3,2,1,0:T(8,128)} async-done(((f32[1,2,128,128]{3,2,1,0:T(8,128)}), f32[8,2,128,128]{3,2,1,0:T(8,128)}) %all-gather.8.cloned.1.call-update) | async-done | bytes 1048592 | tf_op jit(solution)/shard_map/all_gather | solution.py:11
  39.2 25.4 %all-gather.10.cloned.1.call-done = f32[16,128,128]{2,1,0:T(8,128)} async-done(((f32[2,128,128]{2,1,0:T(8,128)}), f32[16,128,128]{2,1,0:T(8,128)}) %all-gather.10.cloned.1.call-update) | async-done | bytes 1048592 | tf_op jit(solution)/shard_map/all_gather | solution.py:11
  64.6 41.8 %while.30 = (s32[]{:T(128)}, f32[2,128,128]{2,1,0:T(8,128)S(1)}, s32[]{:T(128)}, f32[8,2,128,128]{3,2,1,0:T(8,128)}, f32[8,2,128,128]{3,2,1,0:T(8,128)}, /*index=5*/s32[]{:T(128)}, s32[]{:T(128)}, s32[]{}) while((s32[]{:T(128)}, f32[2,128,128]{2,1,0:T(8,128)S(1)}, s32[]{:T(128)}, f32[8,2,128,128]{3,2,1,0:T(8,128)}, ...), condition=%wide.region_1.2_spmd.clone, body=%wide.region_0.1_spmd.clone.sunk | while | flops 100859904 | bytes 1706114 | solution.py:22
  64.6 1.0 fusion.112
  65.6 1.0 fusion.113
  67.7 1.1 fusion.111
  69.8 1.1 fusion.112
  70.8 1.0 fusion.113
  71.9 1.0 fusion.110
  73.0 1.1 fusion.111
  76.1 1.1 fusion.113
  77.1 1.0 fusion.110
  78.2 1.1 fusion.111
  80.2 1.0 fusion.112
  81.3 1.0 fusion.113
  83.4 1.1 fusion.111
  85.5 1.0 fusion.112
  86.5 1.0 fusion.113
  88.6 1.1 fusion.111
  90.7 1.0 fusion.112
  91.7 1.0 fusion.113
  92.8 1.0 fusion.110
  93.9 1.0 fusion.111
  95.9 1.0 fusion.112
  97.0 1.0 fusion.113
  98.0 1.0 fusion.110
  99.1 1.0 fusion.111
  101.1 1.0 fusion.112
  102.2 1.0 fusion.113
  103.2 1.0 fusion.110
  104.3 1.0 fusion.111
  110.1 22.3 %all-gather.14.cloned.1.call-done = f32[16,128,128]{2,1,0:T(8,128)} async-done(((f32[2,128,128]{2,1,0:T(8,128)}), f32[16,128,128]{2,1,0:T(8,128)}) %all-gather.14.cloned.1.call-update) | async-done | bytes 1048592 | tf_op jit(solution)/shard_map/all_gather | solution.py:11
  132.4 41.8 %while.31 = (s32[]{:T(128)}, f32[2,128,128]{2,1,0:T(8,128)S(1)}, s32[]{:T(128)}, f32[8,2,128,128]{3,2,1,0:T(8,128)}, f32[8,2,128,128]{3,2,1,0:T(8,128)}, /*index...) while((s32[]{:T(128)}, f32[2,128,128]{2,1,0:T(8,128)S(1)}, s32[]{:T(128)}, ...), condition=%wide.region_3.4_spmd.clone, body=%wide.region_2.3_spmd.clone.sunk | while | flops 100859912 | bytes 1704144 | solution.py:22
  133.5 1.0 fusion.118
  134.6 1.0 fusion.115
  135.6 1.0 fusion.116
  138.7 1.1 fusion.118
  140.8 1.1 fusion.116
  142.9 1.0 fusion.117
  144.0 1.0 fusion.118
  146.1 1.1 fusion.116
  148.1 1.0 fusion.117
  149.2 1.0 fusion.118
  150.3 1.0 fusion.115
  151.3 1.0 fusion.116
  154.4 1.1 fusion.118
  156.5 1.0 fusion.116
  159.7 1.1 fusion.118
  161.8 1.1 fusion.116
  164.9 1.0 fusion.118
  167.0 1.0 fusion.116
  169.1 1.0 fusion.117
  170.1 1.1 fusion.118
  171.2 1.0 fusion.115
  172.2 1.1 fusion.116
  176.7 2.0 fusion.29
  178.8 35.4 %all-reduce.4.cloned.1.call-done = f32[1,512,128]{2,1,0:T(8,128)} async-done(((f32[1,512,128]{2,1,0:T(8,128)}), f32[1,512,128]{2,1,0:T(8,128)}) %all-reduce.4.cloned.1.call-update) | async-done | bytes 262160 | tf_op jit(solution)/shard_map/psum | solution.py:160
  214.2 1.6 slice_bitcast_fusion.24
  215.9 1.3 collective-permute-start
  217.2 1.3 fusion.22
  218.4 1.2 fusion.36
  221.1 53.6 %all-reduce.6.cloned.1.call-done = (f32[128,128]{1,0:T(8,128)}, f32[128,128]{0,1:T(8,128)}) async-done(((f32[128,128]{1,0:T(8,128)}, f32[128,128]{0,1:T(8,128)}), (f32[128,128]{1,0:T(8,128)}, f32[128,128]{0,1:T(8,128)})) %all-reduce.6.cloned.1.call-update) | async-done | bytes 131088 | tf_op jit(solution)/shard_map/psum | solution.py:164
  (119 shorter events, 44.9 us)
Async XLA Ops:
  7.2 210.0 %copy-start = (f32[1,512,512]{2,1,0:T(8,128)S(1)}, f32[1,512,512]{2,1,0:T(8,128)}, u32[]{:S(2)}) copy-start(f32[1,512,512]{2,1,0:T(8,128)} %param.10) | copy-start | bytes 3145732
  7.2 32.0 %all-gather.8.cloned.1.call-start = ((), (), s32[]{:S(2)}) async-start(), calls=%async_computation | async-start | bytes 1179648 | tf_op jit(solution)/shard_map/all_gather | solution.py:11
  7.2 1.2 copy-start.1
  7.2 2.2 copy-start.7
  11.4 2.6 copy-start.2
  12.8 51.8 %all-gather.10.cloned.1.call-start = ((), (), s32[]{:S(2)}) async-start(), calls=%async_computation.2 | async-start | bytes 1179648 | tf_op jit(solution)/shard_map/all_gather | solution.py:11
  13.9 96.2 %all-gather.12.cloned.1.call-start = ((), (), s32[]{:S(2)}) async-start(), calls=%async_computation.3 | async-start | bytes 1179648 | tf_op jit(solution)/shard_map/all_gather | solution.py:11
  15.8 116.6 %all-gather.14.cloned.1.call-start = ((), (), s32[]{:S(2)}) async-start(), calls=%async_computation.4 | async-start | bytes 1179648 | tf_op jit(solution)/shard_map/all_gather | solution.py:11
  107.4 0.7 copy-start.4
  108.8 105.5 %all-reduce.4.cloned.1.call-start = ((), (), s32[]{:S(2)}) async-start(), calls=%async_computation.1 | async-start | bytes 524288 | tf_op jit(solution)/shard_map/psum | solution.py:160
  108.8 0.7 copy-start.9
  175.7 1.0 copy-start.5
  178.7 96.0 %all-reduce.6.cloned.1.call-start = ((), (), s32[]{:S(2)}) async-start(), calls=%async_computation.5 | async-start | bytes 262144 | tf_op jit(solution)/shard_map/psum | solution.py:164
  214.2 2.9 %copy-start.3 = (f32[1,512,128]{2,1,0:T(8,128)S(1)}, f32[1,512,128]{2,1,0:T(8,128)}, u32[]{:S(2)}) copy-start(f32[1,512,128]{2,1,0:T(8,128)} %all-reduce.4.cloned.1.call-done) | copy-start | bytes 786436
  215.9 3.8 %collective-permute-start = (f32[128,128]{1,0:T(8,128)S(1)}, f32[128,128]{1,0:T(8,128)S(1)}, u32[]{:S(2)}, u32[]{:S(2)}) collective-permute-start(f32[128,128]{1,0:T(8,128)S(1)} %get-tuple-element.289), channel_id=1, source_target_pairs={{1,0},{2,1},{3,2},{4,3},{5,4},{6,5},{7,6},{9,8},{10,9},{11,10},{12... | collective-permute-start | bytes 196616 | tf_op jit(solution)/shard_map/ppermute | solution.py:28
  274.7 1.0 copy-start.6
  274.7 1.0 copy-start.8
Sparse Core Ops, SparseCore 0:
  12.9 26.1 all-gather.7
  41.0 23.4 all-gather.9
  66.5 23.5 all-gather.11
  108.9 23.4 all-gather.13
  178.9 35.3 all-reduce.3
  221.2 53.4 all-reduce.5
where the time goes:
time: 287 us; the launch traced here: 283 us
  waiting for transfers between devices  160 us (56%)
  matrix products  79.8 us (28%)
  other arithmetic  20.9 us (7%)
  between operations  14.5 us (5%)
  local copies, waits for them, and re-layouts  5.19 us (2%)
    all_gather x4, waiting for transfers between devices, prefix(): everything = jax.tree.map(lambda part: lax.all_gather(part, axis), x)  71 us
    psum x1, waiting for transfers between devices, per_device(): gram_total, weighted_total = lax.psum((gram_part, weighted_part), 'slab')  53.6 us
    psum x1, waiting for transfers between devices, per_device(): whole = lax.psum(summed, 'quad')  35.4 us
    dot_general x20, matrix products, complex_times(): jnp.dot(left_cols[1], right_cols[1], precision=precise, preferred_element...  17.7 us
    dot_general x20, matrix products, complex_times(): jnp.dot(left_cols[1], right_cols[0], precision=precise, preferred_element...  17.7 us
    dot_general x20, matrix products, complex_times(): jnp.dot(left_cols[0], right_cols[1], precision=precise, preferred_element...  17.7 us
    dot_general x20, matrix products, complex_times(): jnp.dot(left_cols[0], right_cols[0], precision=precise, preferred_element...  17.6 us
    select_n x16, other arithmetic, step(): return jax.tree.map(lambda a, b: jnp.where(reached, a, b), new, before)  15.2 us
  transfers between devices with their start and end apart: 7, of which 5 were waited for; matrix products, arithmetic and copies ran while one was open for 17% of the time, Pallas kernels for 0%

commit v1 on v0

v1 whole, which is shorter than its diff:
```python
import functools

import jax
import jax.numpy as jnp
from jax import lax
from jax.experimental import pallas as pl
from jax.experimental.pallas import tpu as pltpu
from jax.sharding import PartitionSpec as P

MESH = pl.DeviceIdType.MESH
f32, bf16 = jnp.float32, jnp.bfloat16


def split(x):
    high = x.astype(bf16)
    return high, (x - high.astype(f32)).astype(bf16)


def mm(a, b):
    return jnp.dot(a, b, preferred_element_type=f32)


def dot3(a, b):
    (ah, al), (bh, bl) = a, b
    return mm(ah, bh) + (mm(ah, bl) + mm(al, bh))


def nt(a, b):
    return lax.dot_general(a, b, (((1,), (1,)), ((), ())), preferred_element_type=f32)


def tn(a, b):
    return lax.dot_general(a, b, (((0,), (0,)), ((), ())), preferred_element_type=f32)


def tn3(a, b):
    (ah, al), (bh, bl) = a, b
    return tn(ah, bh) + (tn(ah, bl) + tn(al, bh))


def embed(w):
    n = w.shape[1] // 2
    return split(
        jnp.concatenate([w, jnp.concatenate([-w[:, n:], w[:, :n]], axis=1)], axis=0)
    )


def times(x, e):
    return dot3(split(x), e)


def body(nq, ns, f_hbm, on_hbm, v_hbm, y_hbm, w_ref, sub_ref, corr_ref, proj_ref,
         F, ON, V, Y, onh, onl, maps, vecs, uin, uout, tin, tout, ufull, tfull,
         seg_in, seg_out, z_buf, s_buf, g_buf, s_rs, g_rs, red, red_in, qbuf, full,
         lsem, ssem, rsem):
    B = F.shape[1]
    R = V.shape[0]
    M = Y.shape[1]
    hb = M // 2
    nc = ns // 2
    mid = nc // 2
    qrows = B // nq
    ch = M // ns
    q = lax.axis_index("quad")
    s = lax.axis_index("slab")
    chip = s // 2
    core = s % 2
    buddy = chip * 2 + (1 - core)

    loads = [
        pltpu.make_async_copy(src, dst, lsem.at[i])
        for i, (src, dst) in enumerate(
            [(y_hbm.at[0], Y), (f_hbm.at[0, 0], F), (v_hbm.at[0], V), (on_hbm.at[0], ON)]
        )
    ]
    for copy in loads:
        copy.start()

    barrier = pltpu.get_barrier_semaphore()
    for d in range(1, ns):
        pl.semaphore_signal(barrier, inc=1, device_id={"slab": lax.rem(s + d, ns)}, device_id_type=MESH)
    for d in range(1, nq):
        pl.semaphore_signal(barrier, inc=1, device_id={"quad": lax.rem(q + d, nq)}, device_id_type=MESH)

    def remote(src, dst, sem, **where):
        return pltpu.make_async_remote_copy(
            src_ref=src, dst_ref=dst, send_sem=ssem.at[sem], recv_sem=rsem.at[sem],
            device_id=where, device_id_type=MESH,
        )

    for copy in loads[:3]:
        copy.wait()
    y = Y[...]
    src_re = mm(F[0], y)
    src_im = mm(F[1], y)
    v = V[...]
    vs = split(v)
    vts = split(v.T)
    last = slice(B - R, B)
    f21 = jnp.concatenate([F[0, last, :R], F[1, last, :R]], axis=1)
    a_cols = mm(vts[0], f21) + mm(vts[1], f21)
    s_last = split(jnp.concatenate([src_re[last], src_im[last]], axis=1))
    b_cols = dot3(vts, s_last)
    f12 = jnp.concatenate([F[0, :R, last], F[1, :R, last]], axis=0)
    c_rows = mm(f12, vs[0]) + mm(f12, vs[1])
    vecs[core, 0] = jnp.concatenate([b_cols[:, :M].T, b_cols[:, M:].T], axis=1)
    vecs[core, 1] = jnp.concatenate([src_re[:R].T, src_im[:R].T], axis=1)
    maps[core, 0] = jnp.concatenate([a_cols[:, :R].T, a_cols[:, R:].T], axis=1)
    maps[core, 1] = jnp.concatenate([c_rows[:R].T, c_rows[R:].T], axis=1)
    maps[core, 2] = jnp.concatenate(
        [F[0, :R, :R].astype(f32).T, F[1, :R, :R].astype(f32).T], axis=1
    )

    pl.semaphore_wait(barrier, ns - 1 + nq - 1)
    pair_v = remote(vecs.at[core], vecs.at[core], 0, slab=buddy)
    pair_m = remote(maps.at[core], maps.at[core], 1, slab=buddy)
    pair_v.start()
    pair_m.start()

    wr, wi = w_ref[0, 0], w_ref[0, 1]
    s_buf[...] = wr * src_re - wi * src_im

    pltpu.make_async_remote_copy(
        src_ref=vecs.at[core], dst_ref=vecs.at[1 - core], send_sem=ssem.at[0],
        recv_sem=rsem.at[0], device_id={"slab": buddy}, device_id_type=MESH).wait_recv()
    pltpu.make_async_remote_copy(
        src_ref=maps.at[core], dst_ref=maps.at[1 - core], send_sem=ssem.at[1],
        recv_sem=rsem.at[1], device_id={"slab": buddy}, device_id_type=MESH).wait_recv()

    al, cl, dl = maps[0, 0], maps[0, 1], maps[0, 2]
    ar, cr, dr = maps[1, 0], maps[1, 1], maps[1, 2]
    bl, el = vecs[0, 0], vecs[0, 1]
    br, er = vecs[1, 0], vecs[1, 1]
    zero_map = jnp.zeros((R, 2 * R), f32)
    ab_l = split(jnp.concatenate([al, bl], axis=0))
    ab = dot3(ab_l, embed(ar)) + jnp.concatenate([zero_map, br], axis=0)
    rows = pl.ds(pl.multiple_of(core * hb, hb), hb)
    other_rows = pl.ds(pl.multiple_of((1 - core) * hb, hb), hb)

    def half(x):
        return jnp.where(core == 0, x[:hb], x[hb:])

    forward = remote(uout, uin, 2, slab=jnp.minimum(s + 2, ns - 2 + core))
    back = remote(tout, tin, 3, slab=jnp.maximum(s - 2, core))
    seg = remote(seg_out, seg_in, 4, slab=jnp.maximum(s - 2, core))

    @pl.when(chip == 0)
    def _():
        uin[...] = jnp.zeros_like(uin)
        uout[...] = half(ab[R:])
        forward.start()

    g = dot3(ab_l, embed(dr)) + jnp.concatenate([zero_map, er], axis=0)
    gc = times(jnp.concatenate([g, cr], axis=0), embed(cl))
    chip_d = gc[: R + M] + jnp.concatenate([dl, el], axis=0)
    chip_c = gc[R + M :]

    @pl.when(chip == nc - 1)
    def _():
        z_buf[...] = jnp.zeros_like(z_buf)
        seg_out[...] = chip_d

    @pl.when(jnp.logical_and(chip >= mid, chip < nc - 1))
    def _():
        seg.wait_recv()
        z = times(ab, embed(seg_in[:R])) + jnp.concatenate([zero_map, seg_in[R:]], axis=0)
        z_buf[...] = z
        seg_out[...] = times(z, embed(chip_c)) + chip_d

    @pl.when(chip > mid)
    def _():
        seg.start()

    e_out = embed(ab[:R])
    e_seg = embed(jnp.where(chip >= mid, seg_out[:R], chip_d[:R]))

    @pl.when(chip > 0)
    def _():
        forward.wait_recv()

    u_in = uin[...]
    us = split(u_in)

    @pl.when(chip == mid)
    def _():
        tout[...] = dot3(us, e_seg) + half(seg_out[R:])
        back.start()

    @pl.when(jnp.logical_and(chip > 0, chip < nc - 1))
    def _():
        uout[...] = dot3(us, e_out) + half(ab[R:])
        forward.start()

    ufull[rows, :] = u_in
    cross_u = remote(ufull.at[rows], ufull.at[rows], 5, slab=buddy)
    cross_u.start()

    @pl.when(chip >= mid)
    def _():
        tin[...] = dot3(us, embed(z_buf[:R])) + half(z_buf[R:])

    @pl.when(chip < mid)
    def _():
        const = dot3(us, e_seg) + half(chip_d[R:])
        e_c = embed(chip_c)
        back.wait_recv()

        @pl.when(chip > 0)
        def _():
            tout[...] = times(tin[...], e_c) + const
            back.start()

    tfull[rows, :] = tin[...]
    cross_t = remote(tfull.at[rows], tfull.at[rows], 6, slab=buddy)
    cross_t.start()

    remote(ufull.at[rows], ufull.at[other_rows], 5, slab=buddy).wait_recv()
    u_chip = ufull[...]
    u_left = times(u_chip, embed(al)) + bl
    t_const = times(u_left, embed(dr)) + er
    e_cr = embed(cr)
    u_own = jnp.where(core == 0, u_chip, u_left)

    def weighted(x):
        re, im = x[:, :R], x[:, R:]
        return wr * re - wi * im, -(wr * im + wi * re)

    wu = split(jnp.concatenate(weighted(u_own), axis=1))
    f_left = jnp.concatenate([F[0, :, :R], F[1, :, :R]], axis=1)
    f_right = jnp.concatenate([F[0, :, last], F[1, :, last]], axis=1)
    s_buf[...] += nt(f_left, wu[0]) + nt(f_left, wu[1])
    loads[3].wait()
    on = split(0.5 * ON[...])
    onh[...] = on[0]
    onl[...] = on[1]

    remote(tfull.at[rows], tfull.at[other_rows], 6, slab=buddy).wait_recv()
    t_chip = tfull[...]
    t_own = jnp.where(core == 0, times(t_chip, e_cr) + t_const, t_chip)
    wt = split(jnp.concatenate(weighted(t_own), axis=0))
    vt = nt(wt[0], vs[0]) + (nt(wt[0], vs[1]) + nt(wt[1], vs[0]))
    z = split(jnp.concatenate([vt[:M], vt[M:]], axis=1))
    s_buf[...] += nt(f_right, z[0]) + nt(f_right, z[1])

    base = 7
    quad_copies = []
    for part, (buf, landing) in enumerate([(s_buf, s_rs), (g_buf, g_rs)]):
        if part == 1:
            fs = split(s_buf[...])
            g_buf[...] = dot3((onh[...], onl[...]), fs)
            g_buf[last, :] += vt[:M].T
        for d in range(1, nq):
            to = lax.rem(q + d, nq)
            copy = remote(
                buf.at[pl.ds(pl.multiple_of(to * qrows, qrows), qrows)],
                landing.at[d - 1], base, quad=to)
            copy.start()
            quad_copies.append(copy)
            base += 1
    mine = pl.ds(pl.multiple_of(q * qrows, qrows), qrows)
    total_s = s_buf[mine, :]
    for d in range(1, nq):
        quad_copies[d - 1].wait_recv()
        total_s += s_rs[d - 1]
    sub_ref[0] = total_s
    ss = split(total_s)
    gram = tn3(ss, ss)
    total_g = g_buf[mine, :]
    for d in range(1, nq):
        quad_copies[nq - 2 + d].wait_recv()
        total_g += g_rs[d - 1]
    x = tn3(ss, split(total_g))
    proj = x + x.T

    at_row = lax.broadcasted_iota(jnp.int32, (M, M), 0)
    at_col = lax.broadcasted_iota(jnp.int32, (M, M), 1)
    tile = jnp.where(at_row <= at_col, gram, proj)
    diag = jnp.sum(jnp.where(at_row == at_col, proj, 0.0), axis=0, keepdims=True)
    diag = jnp.broadcast_to(diag, (8, M))
    for i in range(ns):
        red[i, :ch] = tile[i * ch : (i + 1) * ch]
        red[i, ch : ch + 8] = diag
    copies = []
    for d in range(1, ns):
        to = lax.rem(s + d, ns)
        copy = remote(red.at[to], red_in.at[d - 1], base, slab=to)
        copy.start()
        copies.append(copy)
        base += 1
    part = red[s]
    for d in range(1, ns):
        copies[d - 1].wait_recv()
        part += red_in[d - 1]
    qbuf[q] = part
    for d in range(1, nq):
        copy = remote(qbuf.at[q], qbuf.at[q], base, quad=lax.rem(q + d, nq))
        copy.start()
        copies.append(copy)
        base += 1
    for d in range(1, nq):
        remote(qbuf.at[q], qbuf.at[lax.rem(q - d + nq, nq)], base - nq + d, quad=lax.rem(q + d, nq)).wait_recv()
    part = qbuf[0]
    for k in range(1, nq):
        part += qbuf[k]
    full[s] = part
    for d in range(1, ns):
        copy = remote(full.at[s], full.at[s], base, slab=lax.rem(s + d, ns))
        copy.start()
        copies.append(copy)
        base += 1
    for d in range(1, ns):
        remote(full.at[s], full.at[lax.rem(s - d + ns, ns)], base - ns + d, slab=lax.rem(s + d, ns)).wait_recv()
    scale = 1.0 / (ns * B)
    tile = jnp.concatenate([full[i, :ch] for i in range(ns)], axis=0) * scale
    diag = full[0, ch : ch + 1] * scale
    flipped = tile.T
    corr_ref[...] = jnp.where(at_row <= at_col, tile, flipped)
    low = jnp.where(at_row > at_col, tile, flipped)
    proj_ref[...] = jnp.where(at_row == at_col, jnp.broadcast_to(diag, (M, M)), low)

    pair_v.wait_send()
    pair_m.wait_send()
    cross_u.wait_send()
    cross_t.wait_send()

    @pl.when(chip < nc - 1)
    def _():
        forward.wait_send()

    @pl.when(chip > mid)
    def _():
        seg.wait_send()

    @pl.when(jnp.logical_and(chip > 0, chip <= mid))
    def _():
        back.wait_send()

    for copy in quad_copies + copies:
        copy.wait_send()


def per_device(nq, ns, factors, onsite, coupling, vectors, quad_weight):
    B = factors.shape[3]
    R = coupling.shape[1]
    M = vectors.shape[2]
    hb, ch, qrows = M // 2, M // ns, B // nq
    sems = 7 + 2 * (nq - 1) + 2 * (ns - 1) + (nq - 1)
    vm = pltpu.VMEM
    anywhere = pl.BlockSpec(memory_space=pl.ANY)
    here = pl.BlockSpec(memory_space=pltpu.VMEM)
    return pl.pallas_call(
        functools.partial(body, nq, ns),
        out_shape=(
            jax.ShapeDtypeStruct((1, qrows, M), f32),
            jax.ShapeDtypeStruct((M, M), f32),
            jax.ShapeDtypeStruct((M, M), f32),
        ),
        in_specs=[anywhere] * 4 + [pl.BlockSpec(memory_space=pltpu.SMEM)],
        out_specs=(here, here, here),
        scratch_shapes=[
            vm((2, B, B), bf16), vm((B, B), f32), vm((R, R), f32), vm((B, M), bf16),
            vm((B, B), bf16), vm((B, B), bf16),
            vm((2, 3, R, 2 * R), f32), vm((2, 2, M, 2 * R), f32),
            vm((hb, 2 * R), f32), vm((hb, 2 * R), f32), vm((hb, 2 * R), f32), vm((hb, 2 * R), f32),
            vm((M, 2 * R), f32), vm((M, 2 * R), f32),
            vm((R + M, 2 * R), f32), vm((R + M, 2 * R), f32), vm((R + M, 2 * R), f32),
            vm((B, M), f32), vm((B, M), f32),
            vm((nq - 1, qrows, M), f32), vm((nq - 1, qrows, M), f32),
            vm((ns, ch + 8, M), f32), vm((ns - 1, ch + 8, M), f32),
            vm((nq, ch + 8, M), f32), vm((ns, ch + 8, M), f32),
            pltpu.SemaphoreType.DMA((4,)),
            pltpu.SemaphoreType.DMA((sems,)),
            pltpu.SemaphoreType.DMA((sems,)),
        ],
        compiler_params=pltpu.CompilerParams(
            collective_id=0, has_side_effects=True, vmem_limit_bytes=40 * 2**20
        ),
    )(factors, onsite, coupling, vectors, quad_weight)


def solution(mesh):
    placed = (
        P("quad", "slab", None, None, None),
        P("slab", None, None),
        P("slab", None, None),
        P("slab", None, None),
        P("quad", None),
    )
    return jax.shard_map(
        functools.partial(per_device, mesh.shape["quad"], mesh.shape["slab"]),
        mesh=mesh,
        in_specs=placed,
        out_specs=(P("slab", "quad", None), P(), P()),
        check_vma=False,
    )
```

time: 287 us -> 59.9 us (0.21); the launches traced: 283 us -> 59.6 us
  waiting for transfers between devices: 160 us -> 0 us
  matrix products: 79.8 us -> 0 us
  Pallas kernels: 0 us -> 52.2 us
  other arithmetic: 20.9 us -> 0 us
  between operations: 14.5 us -> 0.65 us
    psum x2 -> x0, waiting for transfers between devices: 89.1 us -> none  [the longest x1 53.6 us: per_device(): gram_total, weighted_total = lax.psum((gram_part, weighted_part), 'slab')]
    dot_general x93 -> x0, matrix products: 79.8 us -> none  [the longest x20 17.7 us: complex_times(): jnp.dot(left_cols[1], right_cols[1], precision=precise, preferred_element...]
    all_gather x4 -> x0, waiting for transfers between devices: 71 us -> none  [prefix(): everything = jax.tree.map(lambda part: lax.all_gather(part, axis), x)]
    pallas_call x0 -> x1, Pallas kernels: none -> 52.2 us  [per_device(): pl.pallas_call(functools.partial(body, nq, ns), out_shape=(jax.ShapeDtype...]
    select_n x16 -> x0, other arithmetic: 15.2 us -> none  [step(): return jax.tree.map(lambda a, b: jnp.where(reached, a, b), new, before)]
    unnamed x20 -> x13, local copies, waits for them, and re-layouts: 1.97 us -> 6.73 us
  transfers between devices with their start and end apart: 7 -> 0, of which waited for: 5 -> 0; matrix products, arithmetic and copies ran while one was open for 17% -> 0% of each run, Pallas kernels for 0% -> 0%
where the time goes in v1:
time: 59.9 us; the launch traced here: 59.6 us
  Pallas kernels  52.2 us (87%)
  local copies, waits for them, and re-layouts  6.73 us (11%)
  between operations  0.65 us (1%)
    pallas_call x1, Pallas kernels, per_device(): pl.pallas_call(functools.partial(body, nq, ns), out_shape=(jax.ShapeDtype...  52.2 us
    unnamed x13, local copies, waits for them, and re-layouts  6.73 us

profile of v1, /device:TPU:0, one launch (start us, length us, event | category | flops | bytes accessed | tf_op | source)
XLA Modules:
  0.0 59.6 jit_solution(10175893949020178453)
XLA Ops:
  0.6 0.0 copy-start
  0.6 1.2 %copy-done = bf16[1,1,2,512,512]{4,3,2,1,0:T(8,128)(2,1)S(1)} copy-done((bf16[1,1,2,512,512]{4,3,2,1,0:T(8,128)(2,1)S(1)}, bf16[1,1,2,512,512]{4,3,2,1,0:T(8,128)(2,1)}, u32[]{:S(2)}) %copy-start) | copy-done | bytes 1048600
  1.9 0.0 copy-start.1
  1.9 1.2 %copy-done.1 = f32[1,512,512]{2,1,0:T(8,128)S(1)} copy-done((f32[1,512,512]{2,1,0:T(8,128)S(1)}, f32[1,512,512]{2,1,0:T(8,128)}, u32[]{:S(2)}) %copy-start.1) | copy-done | bytes 1048600
  3.1 0.0 copy-start.2
  3.1 0.9 %copy-done.2 = bf16[1,512,128]{2,1,0:T(8,128)(2,1)S(1)} copy-done((bf16[1,512,128]{2,1,0:T(8,128)(2,1)S(1)}, bf16[1,512,128]{2,1,0:T(8,128)(2,1)}, u32[]{:S(2)}) %copy-start.2) | copy-done | bytes 131096
  4.0 0.0 copy-start.3
  4.0 0.8 %copy-done.3 = f32[1,128,128]{2,1,0:T(8,128)S(1)} copy-done((f32[1,128,128]{2,1,0:T(8,128)S(1)}, f32[1,128,128]{2,1,0:T(8,128)}, u32[]{:S(2)}) %copy-start.3) | copy-done | bytes 65560
  4.8 0.0 copy-start.4
  4.8 0.7 %copy-done.4 = f32[1,2]{1,0:T(1,128)S(1)} copy-done((f32[1,2]{1,0:T(1,128)S(1)}, f32[1,2]{1,0:T(1,128)}, u32[]{:S(2)}) %copy-start.4) | copy-done | bytes 32
  5.5 52.2 %shard_map.76 = (f32[1,128,128]{2,1,0:T(8,128)S(1)}, f32[128,128]{1,0:T(8,128)S(1)}, f32[128,128]{1,0:T(8,128)S(1)}) custom-call(bf16[1,1,2,512,512]{4,3,2,1,0:T(8,128)(2,1)S(1)} %copy-done, f32[1,512,512]{2,1,0:T(8,128)S(1)} %copy-done.1, f32[1,128,128]{2,1,0:T(8,128)S(1)} %copy-done.3, bf16[1,512,128]{2,1,0:T(8,128)(2,1)S(1)} %copy-done.2, ...), custom_call_target="tpu_custom_call" | custom-call | tf_op jit(solution)/shard_map/pallas_call | solution.py:351
  57.7 0.6 %copy.11 = f32[1,128,128]{2,1,0:T(8,128)} copy(f32[1,128,128]{2,1,0:T(8,128)S(1)} %get-tuple-element.6) | data formatting | bytes 131072
  58.4 0.6 %copy.12 = f32[128,128]{1,0:T(8,128)} copy(f32[128,128]{1,0:T(8,128)S(1)} %get-tuple-element.7) | data formatting | bytes 131072
  59.0 0.6 %copy.13 = f32[128,128]{1,0:T(8,128)} copy(f32[128,128]{1,0:T(8,128)S(1)} %get-tuple-element.8) | data formatting | bytes 131072
Async XLA Ops:
  0.6 1.2 %copy-start = (bf16[1,1,2,512,512]{4,3,2,1,0:T(8,128)(2,1)S(1)}, bf16[1,1,2,512,512]{4,3,2,1,0:T(8,128)(2,1)}, u32[]{:S(2)}) copy-start(bf16[1,1,2,512,512]{4,3,2,1,0:T(8,128)(2,1)} %f_hbm.1) | copy-start | bytes 3145732
  1.9 1.2 %copy-start.1 = (f32[1,512,512]{2,1,0:T(8,128)S(1)}, f32[1,512,512]{2,1,0:T(8,128)}, u32[]{:S(2)}) copy-start(f32[1,512,512]{2,1,0:T(8,128)} %on_hbm.1) | copy-start | bytes 3145732
  3.1 0.9 %copy-start.2 = (bf16[1,512,128]{2,1,0:T(8,128)(2,1)S(1)}, bf16[1,512,128]{2,1,0:T(8,128)(2,1)}, u32[]{:S(2)}) copy-start(bf16[1,512,128]{2,1,0:T(8,128)(2,1)} %y_hbm.1) | copy-start | bytes 393220
  4.0 0.8 %copy-start.3 = (f32[1,128,128]{2,1,0:T(8,128)S(1)}, f32[1,128,128]{2,1,0:T(8,128)}, u32[]{:S(2)}) copy-start(f32[1,128,128]{2,1,0:T(8,128)} %v_hbm.1) | copy-start | bytes 196612
  4.8 0.7 %copy-start.4 = (f32[1,2]{1,0:T(1,128)S(1)}, f32[1,2]{1,0:T(1,128)}, u32[]{:S(2)}) copy-start(f32[1,2]{1,0:T(1,128)} %w_ref.1) | copy-start | bytes 28

commit v2 on v1

v2 whole, which is shorter than its diff:
```python
import functools

import jax
import jax.numpy as jnp
from jax import lax
from jax.experimental import pallas as pl
from jax.experimental.pallas import tpu as pltpu
from jax.sharding import PartitionSpec as P

MESH = pl.DeviceIdType.MESH
f32, bf16 = jnp.float32, jnp.bfloat16
VMEM_BYTES = 64 * 2**20 - 64 * 2**10


def split(x):
    high = x.astype(bf16)
    return high, (x - high.astype(f32)).astype(bf16)


def mm(a, b):
    return jnp.dot(a, b, preferred_element_type=f32)


def dot3(a, b):
    (ah, al), (bh, bl) = a, b
    return mm(ah, bh) + (mm(ah, bl) + mm(al, bh))


def nt(a, b):
    return lax.dot_general(a, b, (((1,), (1,)), ((), ())), preferred_element_type=f32)


def tn(a, b):
    return lax.dot_general(a, b, (((0,), (0,)), ((), ())), preferred_element_type=f32)


def tn3(a, b):
    (ah, al), (bh, bl) = a, b
    return tn(ah, bh) + (tn(ah, bl) + tn(al, bh))


def embed(w):
    n = w.shape[1] // 2
    return split(
        jnp.concatenate([w, jnp.concatenate([-w[:, n:], w[:, :n]], axis=1)], axis=0)
    )


def times(x, e):
    return dot3(split(x), e)


def body(nq, ns, f_hbm, on_hbm, v_hbm, y_hbm, w_ref, sub_ref, tile_ref,
         F, ON, V, Y, onh, onl, abs_, cde, uin, uout, tmid, tout, ufull, tfull,
         seg_in, seg_out, z_buf, c_in, c_out, e_in, e_out, s_buf, g_buf, low_in, high_in, nxt, land,
         red, red_in, full, lsem, ssem, rsem):
    B = F.shape[1]
    R = V.shape[0]
    M = Y.shape[1]
    hb = M // 2
    nc = ns // 2
    mid = nc // 2
    qrows = B // nq
    ch = M // ns
    blocks = B // R
    q = lax.axis_index("quad")
    s = lax.axis_index("slab")
    chip = s // 2
    core = s % 2
    buddy = chip * 2 + (1 - core)

    def home(slab):
        return nq // 2 - 1 + slab % 2

    target = home(s)

    loads = [
        pltpu.make_async_copy(src, dst, lsem.at[i])
        for i, (src, dst) in enumerate([
            (y_hbm.at[0], Y), (f_hbm.at[0, 0, 0], F.at[0]), (f_hbm.at[0, 0, 1], F.at[1]),
            (v_hbm.at[0], V), (on_hbm.at[0], ON)])
    ]
    for copy in loads:
        copy.start()

    barrier = pltpu.get_barrier_semaphore()
    for d in range(1, ns):
        pl.semaphore_signal(barrier, inc=1, device_id={"slab": lax.rem(s + d, ns)}, device_id_type=MESH)
    for d in range(1, nq):
        pl.semaphore_signal(barrier, inc=1, device_id={"quad": lax.rem(q + d, nq)}, device_id_type=MESH)

    @pl.when(q == target)
    def _():
        for d in range(1, ns, 2):
            to = lax.rem(s + d, ns)
            pl.semaphore_signal(barrier, inc=1, device_id={"quad": home(to), "slab": to}, device_id_type=MESH)

    counts = [0, 0]

    def fresh(which):
        counts[which] += 1
        return counts[which] - 1

    def remote(src, dst, recv, **where):
        return pltpu.make_async_remote_copy(
            src_ref=src, dst_ref=dst, send_sem=ssem.at[fresh(0)], recv_sem=rsem.at[recv],
            device_id=where, device_id_type=MESH,
        )

    def arrival(dst, recv):
        return pltpu.make_async_remote_copy(
            src_ref=dst, dst_ref=dst, send_sem=ssem.at[0], recv_sem=rsem.at[recv],
            device_id={"slab": buddy}, device_id_type=MESH,
        )

    for copy in loads[:4]:
        copy.wait()
    y = Y[...]
    src_re = mm(F[0], y)
    src_im = mm(F[1], y)
    v = V[...]
    vs = split(v)
    vts = split(v.T)
    last = slice(B - R, B)
    f21 = jnp.concatenate([F[0, last, :R], F[1, last, :R]], axis=1)
    a_cols = mm(vts[0], f21) + mm(vts[1], f21)
    s_last = split(jnp.concatenate([src_re[last], src_im[last]], axis=1))
    b_cols = dot3(vts, s_last)
    abs_[core, :R] = jnp.concatenate([a_cols[:, :R].T, a_cols[:, R:].T], axis=1)
    abs_[core, R:] = jnp.concatenate([b_cols[:, :M].T, b_cols[:, M:].T], axis=1)

    base_wait = ns - 1 + nq - 1

    @pl.when(q == target)
    def _():
        pl.semaphore_wait(barrier, base_wait + ns // 2)

    @pl.when(q != target)
    def _():
        pl.semaphore_wait(barrier, base_wait)

    r_ab, r_cde = fresh(1), fresh(1)
    pair_ab = remote(abs_.at[core], abs_.at[core], r_ab, slab=buddy)
    pair_cde = remote(cde.at[core], cde.at[core], r_cde, slab=buddy)
    pair_ab.start()

    f12 = jnp.concatenate([F[0, :R, last], F[1, :R, last]], axis=0)
    c_rows = mm(f12, vs[0]) + mm(f12, vs[1])
    cde[core, 0] = jnp.concatenate([c_rows[:R].T, c_rows[R:].T], axis=1)
    cde[core, 1] = jnp.concatenate(
        [F[0, :R, :R].astype(f32).T, F[1, :R, :R].astype(f32).T], axis=1
    )
    cde[core, 2] = jnp.concatenate([src_re[:R].T, src_im[:R].T], axis=1)
    pair_cde.start()

    rows = pl.ds(pl.multiple_of(core * hb, hb), hb)
    other_rows = pl.ds(pl.multiple_of((1 - core) * hb, hb), hb)

    def half(x):
        return jnp.where(core == 0, x[:hb], x[hb:])

    r_u, r_t, r_seg, r_relay, r_c, r_e = (fresh(1) for _ in range(6))
    left = jnp.maximum(s - 2, core)
    forward = remote(uout, uin, r_u, slab=jnp.minimum(s + 2, ns - 2 + core))
    back = [remote(tout, tmid, r_t, slab=2 * c + core) for c in range(mid)]
    seg = remote(seg_out.at[core], seg_in.at[core], r_seg, slab=left)
    relay = remote(seg_in.at[core], seg_in.at[core], r_relay, slab=buddy)
    send_c = remote(c_out, c_in, r_c, slab=left)
    send_e = remote(e_out, e_in, r_e, slab=left)
    inner_left = jnp.logical_and(chip > 0, chip < mid)

    arrival(abs_.at[1 - core], r_ab).wait_recv()
    ab_l = split(abs_[0])
    zero_map = jnp.zeros((R, 2 * R), f32)
    ab = dot3(ab_l, embed(abs_[1, :R])) + jnp.concatenate([zero_map, abs_[1, R:]], axis=0)

    @pl.when(chip == 0)
    def _():
        uin[...] = jnp.zeros_like(uin)
        uout[...] = half(ab[R:])
        forward.start()

    arrival(cde.at[1 - core], r_cde).wait_recv()
    cl, dl, el = cde[0, 0], cde[0, 1], cde[0, 2]
    cr, dr, er = cde[1, 0], cde[1, 1], cde[1, 2]
    e_dr = embed(dr)
    g = dot3(ab_l, e_dr) + jnp.concatenate([zero_map, er], axis=0)
    gc = times(jnp.concatenate([g, cr], axis=0), embed(cl))
    chip_d = gc[: R + M] + jnp.concatenate([dl, el], axis=0)
    chip_c = gc[R + M :]

    @pl.when(chip == nc - 1)
    def _():
        z_buf[...] = jnp.zeros_like(z_buf)
        seg_out[0] = chip_d[:R]
        seg_out[1] = chip_d[R:]

    @pl.when(jnp.logical_and(chip >= mid, chip < nc - 1))
    def _():
        seg.wait_recv()
        relay.start()
        arrival(seg_in.at[1 - core], r_relay).wait_recv()
        z = times(ab, embed(seg_in[0])) + jnp.concatenate([zero_map, seg_in[1]], axis=0)
        z_buf[...] = z
        out = times(z, embed(chip_c)) + chip_d
        seg_out[0] = out[:R]
        seg_out[1] = out[R:]

    @pl.when(chip > mid)
    def _():
        seg.start()

    @pl.when(chip == mid - 1)
    def _():
        c_out[...] = chip_c

    @pl.when(chip < mid - 1)
    def _():
        send_c.wait_recv()

        @pl.when(chip > 0)
        def _():
            c_out[...] = times(c_in[...], embed(chip_c))

    @pl.when(inner_left)
    def _():
        send_c.start()

    e_out_map = embed(ab[:R])
    e_seg = embed(jnp.where(chip >= mid, seg_out[0], chip_d[:R]))

    @pl.when(chip > 0)
    def _():
        forward.wait_recv()

    u_in = uin[...]
    us = split(u_in)

    @pl.when(chip == mid)
    def _():
        tout[...] = dot3(us, e_seg) + half(seg_out[1])
        for copy in back:
            copy.start()

    @pl.when(jnp.logical_and(chip > 0, chip < nc - 1))
    def _():
        uout[...] = dot3(us, e_out_map) + half(ab[R:])
        forward.start()

    r_cu, r_ct = fresh(1), fresh(1)
    ufull[rows, :] = u_in
    cross_u = remote(ufull.at[rows], ufull.at[rows], r_cu, slab=buddy)
    cross_u.start()
    cross_t = remote(tfull.at[rows], tfull.at[rows], r_ct, slab=buddy)

    @pl.when(inner_left)
    def _():
        const = dot3(us, e_seg) + half(chip_d[R:])

        @pl.when(chip == mid - 1)
        def _():
            e_out[...] = const

        @pl.when(chip < mid - 1)
        def _():
            send_e.wait_recv()
            e_out[...] = times(e_in[...], embed(chip_c)) + const

        send_e.start()

    @pl.when(chip == 0)
    def _():
        if mid > 1:
            send_e.wait_recv()

    @pl.when(chip >= mid)
    def _():
        tfull[rows, :] = dot3(us, embed(z_buf[:R])) + half(z_buf[R:])
        cross_t.start()

    wr, wi = w_ref[0, 0], w_ref[0, 1]

    def weighted(x):
        re, im = x[:, :R], x[:, R:]
        return wr * re - wi * im, -(wr * im + wi * re)

    arrival(ufull.at[other_rows], r_cu).wait_recv()
    u_chip = ufull[...]
    u_left = times(u_chip, embed(abs_[0, :R])) + abs_[0, R:]
    t_const = times(u_left, e_dr) + er
    e_cr = embed(cr)
    u_own = jnp.where(core == 0, u_chip, u_left)
    wu = split(jnp.concatenate(weighted(u_own), axis=1))
    f_left = jnp.concatenate([F[0, :, :R], F[1, :, :R]], axis=1)
    f_right = jnp.concatenate([F[0, :, last], F[1, :, last]], axis=1)
    s_buf[...] = wr * src_re - wi * src_im + (nt(f_left, wu[0]) + nt(f_left, wu[1]))
    loads[4].wait()

    @pl.when(q == target)
    def _():
        on = split(0.5 * ON[...])
        onh[...] = on[0]
        onl[...] = on[1]

    @pl.when(chip < mid)
    def _():
        back[0].wait_recv()

        @pl.when(chip == mid - 1)
        def _():
            tfull[rows, :] = tmid[...]

        @pl.when(chip < mid - 1)
        def _():
            tfull[rows, :] = times(tmid[...], embed(c_in[...])) + e_in[...]

        cross_t.start()

    arrival(tfull.at[other_rows], r_ct).wait_recv()
    t_chip = tfull[...]
    t_own = jnp.where(core == 0, times(t_chip, e_cr) + t_const, t_chip)
    wt = split(jnp.concatenate(weighted(t_own), axis=0))
    vt = nt(wt[0], vs[0]) + (nt(wt[0], vs[1]) + nt(wt[1], vs[0]))
    z = split(jnp.concatenate([vt[:M], vt[M:]], axis=1))

    ups, downs, r_low, r_high = [], [], [], []
    for i in range(blocks):
        part = slice(i * R, (i + 1) * R)
        r_low.append(fresh(1))
        r_high.append(fresh(1))
        ups.append(remote(s_buf.at[part], low_in.at[i], r_low[i], quad=jnp.minimum(q + 1, nq - 1)))
        downs.append(remote(s_buf.at[part], high_in.at[i], r_high[i], quad=jnp.maximum(q - 1, 0)))
    for i in range(blocks):
        part = slice(i * R, (i + 1) * R)
        s_buf[part, :] += nt(f_right[part], z[0]) + nt(f_right[part], z[1])

        @pl.when(q == 0)
        def _():
            ups[i].start()

        @pl.when(q == nq - 1)
        def _():
            downs[i].start()

    for i in range(blocks):
        part = slice(i * R, (i + 1) * R)

        @pl.when(jnp.logical_and(q > 0, q < target))
        def _():
            ups[i].wait_recv()
            s_buf[part, :] += low_in[i]
            ups[i].start()

        @pl.when(jnp.logical_and(q > target, q < nq - 1))
        def _():
            downs[i].wait_recv()
            s_buf[part, :] += high_in[i]
            downs[i].start()

    r_next, r_sub, r_line, r_full = (fresh(1) for _ in range(4))
    before = jnp.where(s > 0, s - 1, 1)
    to_prev = remote(s_buf.at[:R], nxt, r_next, quad=home(before), slab=before)
    shares = [
        remote(s_buf.at[slice(p * qrows, (p + 1) * qrows)], land, r_sub, quad=p)
        for p in range(nq)
    ]
    r_red = [fresh(1) for _ in range(1, ns)]
    scatter = []
    for d in range(1, ns):
        to = lax.rem(s + d, ns)
        scatter.append(remote(red.at[to], red_in.at[d - 1], r_red[d - 1], quad=home(to), slab=to))
    line = [remote(full.at[s], full.at[s], r_line, quad=lax.rem(q + d, nq)) for d in range(1, nq)]

    @pl.when(q == target)
    def _():
        gram = jnp.zeros((M, M), f32)
        for i in range(blocks):
            part = slice(i * R, (i + 1) * R)
            ups[i].wait_recv()
            downs[i].wait_recv()
            total = s_buf[part, :] + low_in[i] + high_in[i]
            s_buf[part, :] = total
            if i == 0:
                @pl.when(s > 0)
                def _():
                    to_prev.start()
            for p in range(nq):
                if i * R < (p + 1) * qrows <= (i + 1) * R:
                    @pl.when(q == p)
                    def _():
                        land[...] = s_buf[p * qrows : (p + 1) * qrows]

                    @pl.when(q != p)
                    def _():
                        shares[p].start()
            piece = split(total)
            gram += tn3(piece, piece)
            more = dot3((onh[:, part], onl[:, part]), piece)
            if i == 0:
                g_buf[...] = more
            else:
                g_buf[...] += more

        @pl.when(s < ns - 1)
        def _():
            to_prev.wait_recv()
            g_buf[last, :] += dot3(vs, split(nxt[...]))

        x = tn3(split(s_buf[...]), split(g_buf[...]))
        proj = x + x.T

        at_row = lax.broadcasted_iota(jnp.int32, (M, M), 0)
        at_col = lax.broadcasted_iota(jnp.int32, (M, M), 1)
        tile = jnp.where(at_row <= at_col, gram, proj)
        diag = jnp.sum(jnp.where(at_row == at_col, proj, 0.0), axis=0, keepdims=True)
        diag = jnp.broadcast_to(diag, (8, M))
        for i in range(ns):
            red[i, :ch] = tile[i * ch : (i + 1) * ch]
            red[i, ch : ch + 8] = diag
        for copy in scatter:
            copy.start()
        part = red[s]
        for d in range(1, ns):
            scatter[d - 1].wait_recv()
            part += red_in[d - 1]
        full[s] = part
        for copy in line:
            copy.start()

    @pl.when(q != target)
    def _():
        arrival(full.at[s], r_line).wait_recv()
        shares[0].wait_recv()

    spread, r_spread = [], []
    for d in range(1, ns):
        r_spread.append(fresh(1))
        copy = remote(full.at[s], full.at[s], r_spread[-1], slab=lax.rem(s + d, ns))
        copy.start()
        spread.append(copy)
    sub_ref[0] = land[...]
    for d in range(1, ns):
        arrival(full.at[lax.rem(s - d + ns, ns)], r_spread[d - 1]).wait_recv()
    scale = 1.0 / (ns * B)
    for i in range(ns):
        tile_ref[i * ch : (i + 1) * ch, :] = full[i, :ch] * scale
    tile_ref[M : M + 8, :] = full[0, ch : ch + 8] * scale

    for copy in [pair_ab, pair_cde, cross_u, cross_t] + spread:
        copy.wait_send()

    @pl.when(chip < nc - 1)
    def _():
        forward.wait_send()

    @pl.when(chip > mid)
    def _():
        seg.wait_send()

    @pl.when(jnp.logical_and(chip >= mid, chip < nc - 1))
    def _():
        relay.wait_send()

    @pl.when(inner_left)
    def _():
        send_c.wait_send()
        send_e.wait_send()

    @pl.when(chip == mid)
    def _():
        for copy in back:
            copy.wait_send()

    @pl.when(q < target)
    def _():
        for copy in ups:
            copy.wait_send()

    @pl.when(q > target)
    def _():
        for copy in downs:
            copy.wait_send()

    @pl.when(q == target)
    def _():
        for copy in scatter + line:
            copy.wait_send()

        @pl.when(s > 0)
        def _():
            to_prev.wait_send()

        for p in range(nq):
            @pl.when(q != p)
            def _():
                shares[p].wait_send()


def unpack(sub_ref, tile_ref, out_ref, corr_ref, proj_ref):
    M = corr_ref.shape[0]
    out_ref[...] = sub_ref[...]
    tile = tile_ref[:M]
    diag = tile_ref[M : M + 1]
    at_row = lax.broadcasted_iota(jnp.int32, (M, M), 0)
    at_col = lax.broadcasted_iota(jnp.int32, (M, M), 1)
    flipped = tile.T
    corr_ref[...] = jnp.where(at_row <= at_col, tile, flipped)
    low = jnp.where(at_row > at_col, tile, flipped)
    proj_ref[...] = jnp.where(at_row == at_col, jnp.broadcast_to(diag, (M, M)), low)


def per_device(nq, ns, factors, onsite, coupling, vectors, quad_weight):
    B = factors.shape[3]
    R = coupling.shape[1]
    M = vectors.shape[2]
    hb, ch, qrows, blocks = M // 2, M // ns, B // nq, B // R
    sends = 10 + ns // 4 + 2 * blocks + 1 + nq + (ns - 1) + (nq - 1) + (ns - 1)
    recvs = 10 + 2 * blocks + 4 + 2 * (ns - 1)
    vm = pltpu.VMEM
    in_hbm = pl.BlockSpec(memory_space=pltpu.HBM)
    here = pl.BlockSpec(memory_space=pltpu.VMEM)
    wide = vm((M, 2 * R), f32)
    thin = vm((hb, 2 * R), f32)
    sub, tile = pl.pallas_call(
        functools.partial(body, nq, ns),
        out_shape=(
            jax.ShapeDtypeStruct((1, qrows, M), f32),
            jax.ShapeDtypeStruct((M + 8, M), f32),
        ),
        in_specs=[in_hbm] * 4 + [pl.BlockSpec(memory_space=pltpu.SMEM)],
        out_specs=(here, here),
        scratch_shapes=[
            vm((2, B, B), bf16), vm((B, B), f32), vm((R, R), f32), vm((B, M), bf16),
            vm((B, B), bf16), vm((B, B), bf16),
            vm((2, R + M, 2 * R), f32), vm((2, 3, R, 2 * R), f32),
            thin, thin, thin, thin, wide, wide,
            vm((2, R, 2 * R), f32), vm((2, R, 2 * R), f32), vm((R + M, 2 * R), f32),
            vm((R, 2 * R), f32), vm((R, 2 * R), f32), thin, thin,
            vm((B, M), f32), vm((B, M), f32),
            vm((blocks, R, M), f32), vm((blocks, R, M), f32), vm((R, M), f32), vm((qrows, M), f32),
            vm((ns, ch + 8, M), f32), vm((ns - 1, ch + 8, M), f32), vm((ns, ch + 8, M), f32),
            pltpu.SemaphoreType.DMA((5,)),
            pltpu.SemaphoreType.DMA((sends,)),
            pltpu.SemaphoreType.DMA((recvs,)),
        ],
        compiler_params=pltpu.CompilerParams(
            collective_id=0, has_side_effects=True, vmem_limit_bytes=VMEM_BYTES
        ),
    )(factors, onsite, coupling, vectors, quad_weight)
    return pl.pallas_call(
        unpack,
        out_shape=(
            jax.ShapeDtypeStruct((1, qrows, M), f32),
            jax.ShapeDtypeStruct((M, M), f32),
            jax.ShapeDtypeStruct((M, M), f32),
        ),
        in_specs=[here, here],
        out_specs=(here, here, here),
        compiler_params=pltpu.CompilerParams(vmem_limit_bytes=VMEM_BYTES),
    )(sub, tile)


def solution(mesh):
    placed = (
        P("quad", "slab", None, None, None),
        P("slab", None, None),
        P("slab", None, None),
        P("slab", None, None),
        P("quad", None),
    )
    return jax.shard_map(
        functools.partial(per_device, mesh.shape["quad"], mesh.shape["slab"]),
        mesh=mesh,
        in_specs=placed,
        out_specs=(P("slab", "quad", None), P(), P()),
        check_vma=False,
    )
```

time: 59.9 us -> 48.5 us (0.81)
  local copies, waits for them, and re-layouts: 6.73 us -> 0 us
  Pallas kernels: 52.2 us -> 47.7 us
    unnamed x13 -> x0, local copies, waits for them, and re-layouts: 6.73 us -> none
    pallas_call x1, Pallas kernels: 52.2 us -> 46 us  [per_device(): pl.pallas_call(functools.partial(body, nq, ns), out_shape=(jax.ShapeDtype...]
    pallas_call x0 -> x1, Pallas kernels: none -> 1.68 us  [per_device(): pl.pallas_call(unpack, out_shape=(jax.ShapeDtypeStruct((1, qrows, M), f32...]
where the time goes in v2:
time: 48.5 us; the launch traced here: 48.3 us
  Pallas kernels  47.7 us (98%)
  between operations  0.64 us (1%)
    pallas_call x1, Pallas kernels, per_device(): pl.pallas_call(functools.partial(body, nq, ns), out_shape=(jax.ShapeDtype...  46 us
    pallas_call x1, Pallas kernels, per_device(): pl.pallas_call(unpack, out_shape=(jax.ShapeDtypeStruct((1, qrows, M), f32...  1.68 us

profile of v2, /device:TPU:0, one launch (start us, length us, event | category | flops | bytes accessed | tf_op | source)
XLA Modules:
  0.0 48.3 jit_solution(13346558357004150930)
XLA Ops:
  0.6 46.0 %shard_map.76 = (f32[1,128,128]{2,1,0:T(8,128)}, f32[136,128]{1,0:T(8,128)}) custom-call(bf16[1,1,2,512,512]{4,3,2,1,0:T(8,128)(2,1)} %f_hbm.1, f32[1,512,512]{2,1,0:T(8,128)} %on_hbm.1, f32[1,128,128]{2,1,0:T(8,128)} %v_hbm.1, bf16[1,512,128]{2,1,0:T(8,128)(2,1)} %y_hbm.1, f32[1,2]{1,0:T(1,128)} %w_ref.1), custom_call_target="tpu_custom_call" | custom-call | tf_op jit(solution)/shard_map/pallas_call | solution.py:524
  46.6 1.7 %shard_map.77 = (f32[1,128,128]{2,1,0:T(8,128)}, f32[128,128]{1,0:T(8,128)}, f32[128,128]{1,0:T(8,128)}) custom-call(f32[1,128,128]{2,1,0:T(8,128)} %get-tuple-element.5.sub_ref, f32[136,128]{1,0:T(8,128)} %get-tuple-element.6.tile_ref), custom_call_target="tpu_custom_call" | custom-call | tf_op jit(solution)/shard_map/pallas_call | solution.py:550

commit v3 on v2

v3 whole, which is shorter than its diff:
```python
import functools

import jax
import jax.numpy as jnp
from jax import lax
from jax.experimental import pallas as pl
from jax.experimental.pallas import tpu as pltpu
from jax.sharding import PartitionSpec as P

MESH = pl.DeviceIdType.MESH
f32, bf16 = jnp.float32, jnp.bfloat16
VMEM_BYTES = 64 * 2**20 - 64 * 2**10


def split(x):
    high = x.astype(bf16)
    return high, (x - high.astype(f32)).astype(bf16)


def mm(a, b):
    return jnp.dot(a, b, preferred_element_type=f32)


def dot3(a, b):
    (ah, al), (bh, bl) = a, b
    return mm(ah, bh) + (mm(ah, bl) + mm(al, bh))


def nt(a, b):
    return lax.dot_general(a, b, (((1,), (1,)), ((), ())), preferred_element_type=f32)


def tn(a, b):
    return lax.dot_general(a, b, (((0,), (0,)), ((), ())), preferred_element_type=f32)


def tn3(a, b):
    (ah, al), (bh, bl) = a, b
    return tn(ah, bh) + (tn(ah, bl) + tn(al, bh))


def embed(w):
    n = w.shape[1] // 2
    return split(
        jnp.concatenate([w, jnp.concatenate([-w[:, n:], w[:, :n]], axis=1)], axis=0)
    )


def times(x, e):
    return dot3(split(x), e)


def body(nq, ns, f_hbm, on_hbm, v_hbm, y_hbm, w_ref, sub_ref, tile_ref,
         F, ON, V, Y, onh, onl, abs_, cde, uin, uout, tmid, tout, ufull, t_buf,
         dm_in, dm_out, dv_in, dv_out, c_in, c_out, e_in, e_out, s_buf, b_in, p_out, p_in, ph, pl_,
         wt_out, wt_in, land, red, red_in, full, lsem, ssem, rsem):
    B = F.shape[1]
    R = V.shape[0]
    M = Y.shape[1]
    hb = M // 2
    nc = ns // 2
    mid = nc // 2
    qrows = B // nq
    ch = M // ns
    q = lax.axis_index("quad")
    s = lax.axis_index("slab")
    chip = s // 2
    core = s % 2
    buddy = chip * 2 + (1 - core)

    def home(slab):
        return nq // 2 - 1 + slab % 2

    target = home(s)

    top, last = slice(0, B - R), slice(B - R, B)
    loads = [
        pltpu.make_async_copy(src, dst, lsem.at[i])
        for i, (src, dst) in enumerate([
            (y_hbm.at[0], Y), (v_hbm.at[0], V),
            (f_hbm.at[0, 0, 0, last], F.at[0, last]), (f_hbm.at[0, 0, 1, last], F.at[1, last]),
            (f_hbm.at[0, 0, 0, top], F.at[0, top]), (f_hbm.at[0, 0, 1, top], F.at[1, top]),
            (on_hbm.at[0], ON)])
    ]
    for copy in loads:
        copy.start()

    barrier = pltpu.get_barrier_semaphore()
    for d in range(1, ns):
        pl.semaphore_signal(barrier, inc=1, device_id={"slab": lax.rem(s + d, ns)}, device_id_type=MESH)
    for d in range(1, nq):
        pl.semaphore_signal(barrier, inc=1, device_id={"quad": lax.rem(q + d, nq)}, device_id_type=MESH)
        pl.semaphore_signal(
            barrier, inc=1, device_id={"quad": lax.rem(q + d, nq), "slab": buddy}, device_id_type=MESH)

    @pl.when(q == target)
    def _():
        for d in range(2, ns, 2):
            to = lax.rem(buddy + d, ns)
            pl.semaphore_signal(barrier, inc=1, device_id={"quad": home(to), "slab": to}, device_id_type=MESH)

    counts = [0, 0]

    def fresh(which):
        counts[which] += 1
        return counts[which] - 1

    def remote(src, dst, recv, **where):
        return pltpu.make_async_remote_copy(
            src_ref=src, dst_ref=dst, send_sem=ssem.at[fresh(0)], recv_sem=rsem.at[recv],
            device_id=where, device_id_type=MESH,
        )

    def arrival(dst, recv):
        return pltpu.make_async_remote_copy(
            src_ref=dst, dst_ref=dst, send_sem=ssem.at[0], recv_sem=rsem.at[recv],
            device_id={"slab": buddy}, device_id_type=MESH,
        )

    for copy in loads[:4]:
        copy.wait()
    y = Y[...]
    last_re = mm(F[0, last], y)
    last_im = mm(F[1, last], y)
    vs = split(V[...])
    vts = split(V[...].T)
    f21 = jnp.concatenate([F[0, last, :R], F[1, last, :R]], axis=1)
    a_cols = mm(vts[0], f21) + mm(vts[1], f21)
    s_last = split(jnp.concatenate([last_re, last_im], axis=1))
    b_cols = dot3(vts, s_last)
    abs_[core, :R] = jnp.concatenate([a_cols[:, :R].T, a_cols[:, R:].T], axis=1)
    abs_[core, R:] = jnp.concatenate([b_cols[:, :M].T, b_cols[:, M:].T], axis=1)

    base_wait = ns - 1 + 2 * (nq - 1)

    @pl.when(q == target)
    def _():
        pl.semaphore_wait(barrier, base_wait + ns // 2 - 1)

    @pl.when(q != target)
    def _():
        pl.semaphore_wait(barrier, base_wait)

    r_ab, r_cde = fresh(1), fresh(1)
    pair_ab = remote(abs_.at[core], abs_.at[core], r_ab, slab=buddy)
    pair_cde = remote(cde.at[core], cde.at[core], r_cde, slab=buddy)
    pair_ab.start()

    for copy in loads[4:6]:
        copy.wait()
    src_re = jnp.concatenate([mm(F[0, top], y), last_re], axis=0)
    src_im = jnp.concatenate([mm(F[1, top], y), last_im], axis=0)
    f_right = jnp.concatenate([F[0, :, last], F[1, :, last]], axis=0)
    p_rows = mm(f_right, vs[0]) + mm(f_right, vs[1])
    cde[core, 0] = jnp.concatenate([p_rows[:R].T, p_rows[B : B + R].T], axis=1)
    cde[core, 1] = jnp.concatenate(
        [F[0, :R, :R].astype(f32).T, F[1, :R, :R].astype(f32).T], axis=1
    )
    cde[core, 2] = jnp.concatenate([src_re[:R].T, src_im[:R].T], axis=1)
    pair_cde.start()
    p_out[...] = jnp.concatenate([p_rows[:B], p_rows[B:]], axis=1)
    r_p = [fresh(1) for _ in range(1, nq)]
    r_b = [fresh(1) for _ in range(1, nq)]
    r_wt = [fresh(1) for _ in range(2 * nq)]
    away = lax.rem(q - target + nq, nq)
    slot = jnp.maximum(away - 1, 0)
    send_p = remote(p_out, p_in.at[slot], r_p[0] + slot, quad=target)
    send_b = remote(s_buf, b_in.at[slot], r_b[0] + slot, quad=target)

    @pl.when(q != target)
    def _():
        send_p.start()

    rows = pl.ds(pl.multiple_of(core * hb, hb), hb)
    other_rows = pl.ds(pl.multiple_of((1 - core) * hb, hb), hb)

    def half(x):
        return jnp.where(core == 0, x[:hb], x[hb:])

    r_u, r_t, r_dm, r_dv, r_relay, r_c, r_e = (fresh(1) for _ in range(7))
    left = jnp.maximum(s - 2, core)
    forward = remote(uout, uin, r_u, slab=jnp.minimum(s + 2, ns - 2 + core))
    back = [remote(tout, tmid, r_t, slab=2 * c + core) for c in range(mid)]
    send_dm = remote(dm_out.at[rows], dm_in.at[rows], r_dm, slab=left)
    send_dv = remote(dv_out, dv_in, r_dv, slab=left)
    relay = remote(dm_in.at[rows], dm_in.at[rows], r_relay, slab=buddy)
    send_c = remote(c_out, c_in, r_c, slab=left)
    send_e = remote(e_out, e_in, r_e, slab=left)
    inner_left = jnp.logical_and(chip > 0, chip < mid)

    arrival(abs_.at[1 - core], r_ab).wait_recv()
    ab_l = split(abs_[0])
    zero_map = jnp.zeros((R, 2 * R), f32)
    ab = dot3(ab_l, embed(abs_[1, :R])) + jnp.concatenate([zero_map, abs_[1, R:]], axis=0)

    @pl.when(chip == 0)
    def _():
        uin[...] = jnp.zeros_like(uin)
        uout[...] = half(ab[R:])
        forward.start()

    arrival(cde.at[1 - core], r_cde).wait_recv()
    cl, dl, el = cde[0, 0], cde[0, 1], cde[0, 2]
    cr, dr, er = cde[1, 0], cde[1, 1], cde[1, 2]
    e_dr = embed(dr)
    g = dot3(ab_l, e_dr) + jnp.concatenate([zero_map, er], axis=0)
    gc = times(jnp.concatenate([g, cr], axis=0), embed(cl))
    chip_d = gc[: R + M] + jnp.concatenate([dl, el], axis=0)
    chip_c = gc[R + M :]

    d_half = half(chip_d[R:])
    b_half = half(ab[R:])

    @pl.when(chip == nc - 1)
    def _():
        dm_out[...] = chip_d[:R]
        dv_out[...] = d_half
        send_dm.start()
        send_dv.start()

    @pl.when(jnp.logical_and(chip >= mid, chip < nc - 1))
    def _():
        send_dm.wait_recv()
        relay.start()

        @pl.when(chip > mid)
        def _():
            arrival(dm_in.at[other_rows], r_relay).wait_recv()
            z = times(jnp.concatenate([ab[:R], b_half], axis=0), embed(dm_in[...]))
            send_dv.wait_recv()
            z_b = z[R:] + dv_in[...]
            out = times(jnp.concatenate([z[:R], z_b], axis=0), embed(chip_c))
            dm_out[...] = out[:R] + chip_d[:R]
            dv_out[...] = out[R:] + d_half
            send_dm.start()
            send_dv.start()

    @pl.when(chip == mid - 1)
    def _():
        c_out[...] = chip_c

    @pl.when(chip < mid - 1)
    def _():
        send_c.wait_recv()

        @pl.when(chip > 0)
        def _():
            c_out[...] = times(c_in[...], embed(chip_c))

    @pl.when(inner_left)
    def _():
        send_c.start()

    e_out_map = embed(ab[:R])
    e_d = embed(chip_d[:R])
    e_c = embed(chip_c)

    @pl.when(chip > 0)
    def _():
        forward.wait_recv()

    u_in = uin[...]
    us = split(u_in)

    @pl.when(chip == nc - 1)
    def _():
        t_buf[...] = jnp.zeros_like(t_buf)

    @pl.when(jnp.logical_and(chip > 0, chip < nc - 1))
    def _():
        u_out = dot3(us, e_out_map) + b_half
        uout[...] = u_out
        forward.start()

        @pl.when(chip >= mid)
        def _():
            const = dot3(us, e_d) + d_half

            @pl.when(chip == mid)
            def _():
                arrival(dm_in.at[other_rows], r_relay).wait_recv()
                send_dv.wait_recv()

            t_in = times(u_out, embed(dm_in[...])) + dv_in[...]
            t_buf[...] = t_in

            @pl.when(chip == mid)
            def _():
                tout[...] = times(t_in, e_c) + const
                for copy in back:
                    copy.start()

    r_cu = fresh(1)
    ufull[rows, :] = u_in
    cross_u = remote(ufull.at[rows], ufull.at[rows], r_cu, slab=buddy)
    cross_u.start()

    @pl.when(inner_left)
    def _():
        const = dot3(us, e_d) + d_half

        @pl.when(chip == mid - 1)
        def _():
            e_out[...] = const

        @pl.when(chip < mid - 1)
        def _():
            send_e.wait_recv()
            e_out[...] = times(e_in[...], e_c) + const

        send_e.start()

    @pl.when(chip == 0)
    def _():
        if mid > 1:
            send_e.wait_recv()

    wr, wi = w_ref[0, 0], w_ref[0, 1]

    def weighted(x):
        re, im = x[:, :R], x[:, R:]
        return wr * re - wi * im, -(wr * im + wi * re)

    arrival(ufull.at[other_rows], r_cu).wait_recv()
    u_chip = ufull[...]
    e_al = embed(abs_[0, :R])
    e_cr = embed(cr)
    u_left = times(u_chip, e_al) + abs_[0, R:]
    u_own = jnp.where(core == 0, u_chip, u_left)
    wu = split(jnp.concatenate(weighted(u_own), axis=1))
    f_left = jnp.concatenate([F[0, :, :R], F[1, :, :R]], axis=1)
    s_buf[...] = wr * src_re - wi * src_im + (nt(f_left, wu[0]) + nt(f_left, wu[1]))

    @pl.when(q != target)
    def _():
        send_b.start()

    t_const = times(dot3(us, e_al) + half(abs_[0, R:]), e_dr) + half(er)
    loads[6].wait()

    @pl.when(q == target)
    def _():
        on = split(0.5 * ON[...])
        onh[...] = on[0]
        onl[...] = on[1]

    @pl.when(chip < mid)
    def _():
        back[0].wait_recv()

        @pl.when(chip == mid - 1)
        def _():
            t_buf[...] = tmid[...]

        @pl.when(chip < mid - 1)
        def _():
            t_buf[...] = times(tmid[...], embed(c_in[...])) + e_in[...]

    t_in = t_buf[...]
    wt_out[1] = jnp.concatenate(weighted(t_in), axis=1)
    to_home = []
    for k in (1, 0):
        if k == 0:
            wt_out[0] = jnp.concatenate(weighted(times(t_in, e_cr) + t_const), axis=1)
        at = nq // 2 - 1 + k
        hop = lax.rem(q - at + nq, nq)
        mine = jnp.logical_and(q == at, core == k)
        copy = remote(wt_out.at[k], wt_in.at[hop, rows], r_wt[0] + 2 * hop + core,
                      quad=at, slab=jnp.where(mine, buddy, chip * 2 + k))
        to_home.append((mine, copy))

        @pl.when(mine)
        def _():
            wt_in[0, rows] = wt_out[k]

        @pl.when(jnp.logical_not(mine))
        def _():
            copy.start()

    r_sub, r_line = fresh(1), fresh(1)
    shares = [
        remote(s_buf.at[slice(p * qrows, (p + 1) * qrows)], land, r_sub, quad=p)
        for p in range(nq)
    ]
    r_red = [fresh(1) for _ in range(1, ns)]
    scatter = []
    for d in range(1, ns):
        to = lax.rem(s + d, ns)
        scatter.append(remote(red.at[to], red_in.at[d - 1], r_red[d - 1], quad=home(to), slab=to))
    line = [remote(full.at[s], full.at[s], r_line, quad=lax.rem(q + d, nq)) for d in range(1, nq)]

    @pl.when(q == target)
    def _():
        total = s_buf[...]
        for d in range(1, nq):
            arrival(b_in.at[d - 1], r_b[d - 1]).wait_recv()
            total += b_in[d - 1]
        for d in range(nq):
            if d > 0:
                arrival(p_in.at[d - 1], r_p[d - 1]).wait_recv()
            piece = split(p_out[...] if d == 0 else p_in[d - 1])
            ph[:, d * 2 * R : (d + 1) * 2 * R] = piece[0]
            pl_[:, d * 2 * R : (d + 1) * 2 * R] = piece[1]
        for d in range(nq):
            for k in (0, 1):
                if d > 0:
                    arrival(wt_in.at[d, k * hb : (k + 1) * hb], r_wt[2 * d + k]).wait_recv()
                else:
                    @pl.when(core != k)
                    def _():
                        arrival(wt_in.at[0, k * hb : (k + 1) * hb], r_wt[k]).wait_recv()
        zh, zl = split(jnp.concatenate([wt_in[d] for d in range(nq)], axis=1))
        total += nt(ph[...], zh) + (nt(ph[...], zl) + nt(pl_[...], zh))
        s_buf[...] = total
        for p in range(nq):
            @pl.when(q == p)
            def _():
                land[...] = s_buf[p * qrows : (p + 1) * qrows]

            @pl.when(q != p)
            def _():
                shares[p].start()
        ts = split(total)
        half_h = dot3((onh[...], onl[...]), ts)
        following = wt_in[0, :, :R]
        for d in range(1, nq):
            following += wt_in[d, :, :R]
        fs = split(following)
        upper = nt(vs[0], fs[0]) + (nt(vs[0], fs[1]) + nt(vs[1], fs[0]))
        weighted_rows = split(jnp.concatenate([half_h[top], half_h[last] + upper], axis=0))
        both = tuple(jnp.concatenate([a, b], axis=1) for a, b in zip(ts, weighted_rows))
        products = dot3(split(total.T), both)
        gram, x = products[:, :M], products[:, M:]
        proj = x + x.T

        at_row = lax.broadcasted_iota(jnp.int32, (M, M), 0)
        at_col = lax.broadcasted_iota(jnp.int32, (M, M), 1)
        tile = jnp.where(at_row <= at_col, gram, proj)
        diag = jnp.sum(jnp.where(at_row == at_col, proj, 0.0), axis=0, keepdims=True)
        diag = jnp.broadcast_to(diag, (8, M))
        for i in range(ns):
            red[i, :ch] = tile[i * ch : (i + 1) * ch]
            red[i, ch : ch + 8] = diag
        for copy in scatter:
            copy.start()
        part = red[s]
        for d in range(1, ns):
            scatter[d - 1].wait_recv()
            part += red_in[d - 1]
        full[s] = part
        for copy in line:
            copy.start()

    @pl.when(q != target)
    def _():
        arrival(full.at[s], r_line).wait_recv()
        shares[0].wait_recv()

    spread, r_spread = [], []
    for d in range(1, ns):
        r_spread.append(fresh(1))
        copy = remote(full.at[s], full.at[s], r_spread[-1], slab=lax.rem(s + d, ns))
        copy.start()
        spread.append(copy)
    sub_ref[0] = land[...]
    for d in range(1, ns):
        arrival(full.at[lax.rem(s - d + ns, ns)], r_spread[d - 1]).wait_recv()
    scale = 1.0 / (ns * B)
    for i in range(ns):
        tile_ref[i * ch : (i + 1) * ch, :] = full[i, :ch] * scale
    tile_ref[M : M + 8, :] = full[0, ch : ch + 8] * scale

    for copy in [pair_ab, pair_cde, cross_u] + spread:
        copy.wait_send()

    @pl.when(chip < nc - 1)
    def _():
        forward.wait_send()

    @pl.when(chip > mid)
    def _():
        send_dm.wait_send()
        send_dv.wait_send()

    @pl.when(jnp.logical_and(chip >= mid, chip < nc - 1))
    def _():
        relay.wait_send()

    @pl.when(inner_left)
    def _():
        send_c.wait_send()
        send_e.wait_send()

    @pl.when(chip == mid)
    def _():
        for copy in back:
            copy.wait_send()

    for mine, copy in to_home:
        @pl.when(jnp.logical_not(mine))
        def _():
            copy.wait_send()

    @pl.when(q != target)
    def _():
        send_p.wait_send()
        send_b.wait_send()

    @pl.when(q == target)
    def _():
        for copy in scatter + line:
            copy.wait_send()

        for p in range(nq):
            @pl.when(q != p)
            def _():
                shares[p].wait_send()


def unpack(sub_ref, tile_ref, out_ref, corr_ref, proj_ref):
    M = corr_ref.shape[0]
    out_ref[...] = sub_ref[...]
    tile = tile_ref[:M]
    diag = tile_ref[M : M + 1]
    at_row = lax.broadcasted_iota(jnp.int32, (M, M), 0)
    at_col = lax.broadcasted_iota(jnp.int32, (M, M), 1)
    flipped = tile.T
    corr_ref[...] = jnp.where(at_row <= at_col, tile, flipped)
    low = jnp.where(at_row > at_col, tile, flipped)
    proj_ref[...] = jnp.where(at_row == at_col, jnp.broadcast_to(diag, (M, M)), low)


def per_device(nq, ns, factors, onsite, coupling, vectors, quad_weight):
    B = factors.shape[3]
    R = coupling.shape[1]
    M = vectors.shape[2]
    hb, ch, qrows = M // 2, M // ns, B // nq
    sends = 13 + ns // 4 + nq + 2 * (ns - 1) + (nq - 1)
    recvs = 12 + 2 * (nq - 1) + 2 * nq + 2 * (ns - 1)
    vm = pltpu.VMEM
    in_hbm = pl.BlockSpec(memory_space=pltpu.HBM)
    here = pl.BlockSpec(memory_space=pltpu.VMEM)
    wide = vm((M, 2 * R), f32)
    thin = vm((hb, 2 * R), f32)
    sub, tile = pl.pallas_call(
        functools.partial(body, nq, ns),
        out_shape=(
            jax.ShapeDtypeStruct((1, qrows, M), f32),
            jax.ShapeDtypeStruct((M + 8, M), f32),
        ),
        in_specs=[in_hbm] * 4 + [pl.BlockSpec(memory_space=pltpu.SMEM)],
        out_specs=(here, here),
        scratch_shapes=[
            vm((2, B, B), bf16), vm((B, B), f32), vm((R, R), f32), vm((B, M), bf16),
            vm((B, B), bf16), vm((B, B), bf16),
            vm((2, R + M, 2 * R), f32), vm((2, 3, R, 2 * R), f32),
            thin, thin, thin, thin, wide, thin,
            wide, wide, thin, thin, wide, wide, thin, thin,
            vm((B, M), f32), vm((nq - 1, B, M), f32),
            vm((B, 2 * R), f32), vm((nq - 1, B, 2 * R), f32),
            vm((B, 2 * nq * R), bf16), vm((B, 2 * nq * R), bf16),
            vm((2, hb, 2 * R), f32), vm((nq, M, 2 * R), f32), vm((qrows, M), f32),
            vm((ns, ch + 8, M), f32), vm((ns - 1, ch + 8, M), f32), vm((ns, ch + 8, M), f32),
            pltpu.SemaphoreType.DMA((7,)),
            pltpu.SemaphoreType.DMA((sends,)),
            pltpu.SemaphoreType.DMA((recvs,)),
        ],
        compiler_params=pltpu.CompilerParams(
            collective_id=0, has_side_effects=True, vmem_limit_bytes=VMEM_BYTES
        ),
    )(factors, onsite, coupling, vectors, quad_weight)
    return pl.pallas_call(
        unpack,
        out_shape=(
            jax.ShapeDtypeStruct((1, qrows, M), f32),
            jax.ShapeDtypeStruct((M, M), f32),
            jax.ShapeDtypeStruct((M, M), f32),
        ),
        in_specs=[here, here],
        out_specs=(here, here, here),
        compiler_params=pltpu.CompilerParams(vmem_limit_bytes=VMEM_BYTES),
    )(sub, tile)


def solution(mesh):
    placed = (
        P("quad", "slab", None, None, None),
        P("slab", None, None),
        P("slab", None, None),
        P("slab", None, None),
        P("quad", None),
    )
    return jax.shard_map(
        functools.partial(per_device, mesh.shape["quad"], mesh.shape["slab"]),
        mesh=mesh,
        in_specs=placed,
        out_specs=(P("slab", "quad", None), P(), P()),
        check_vma=False,
    )
```

time: 48.5 us -> 46.3 us (0.955)
  Pallas kernels: 47.7 us -> 45.5 us
    pallas_call x1, Pallas kernels: 46 us -> 43.8 us  [per_device(): pl.pallas_call(functools.partial(body, nq, ns), out_shape=(jax.ShapeDtype...]
where the time goes in v3:
time: 46.3 us; the launch traced here: 46.1 us
  Pallas kernels  45.5 us (98%)
  between operations  0.64 us (1%)
    pallas_call x1, Pallas kernels, per_device(): pl.pallas_call(functools.partial(body, nq, ns), out_shape=(jax.ShapeDtype...  43.8 us
    pallas_call x1, Pallas kernels, per_device(): pl.pallas_call(unpack, out_shape=(jax.ShapeDtypeStruct((1, qrows, M), f32...  1.68 us

profile of v3, /device:TPU:0, one launch (start us, length us, event | category | flops | bytes accessed | tf_op | source)
XLA Modules:
  0.0 46.1 jit_solution(6460086780051620507)
XLA Ops:
  0.6 43.8 %shard_map.76 = (f32[1,128,128]{2,1,0:T(8,128)}, f32[136,128]{1,0:T(8,128)}) custom-call(bf16[1,1,2,512,512]{4,3,2,1,0:T(8,128)(2,1)} %f_hbm.1, f32[1,512,512]{2,1,0:T(8,128)} %on_hbm.1, f32[1,128,128]{2,1,0:T(8,128)} %v_hbm.1, bf16[1,512,128]{2,1,0:T(8,128)(2,1)} %y_hbm.1, f32[1,2]{1,0:T(1,128)} %w_ref.1), custom_call_target="tpu_custom_call" | custom-call | tf_op jit(solution)/shard_map/pallas_call | solution.py:545
  44.4 1.7 %shard_map.77 = (f32[1,128,128]{2,1,0:T(8,128)}, f32[128,128]{1,0:T(8,128)}, f32[128,128]{1,0:T(8,128)}) custom-call(f32[1,128,128]{2,1,0:T(8,128)} %get-tuple-element.5.sub_ref, f32[136,128]{1,0:T(8,128)} %get-tuple-element.6.tile_ref), custom_call_target="tpu_custom_call" | custom-call | tf_op jit(solution)/shard_map/pallas_call | solution.py:572

commit v4 on v3

--- a/solution.py
+++ b/solution.py
@@ -52,8 +52,8 @@
 
 def body(nq, ns, f_hbm, on_hbm, v_hbm, y_hbm, w_ref, sub_ref, tile_ref,
          F, ON, V, Y, onh, onl, abs_, cde, uin, uout, tmid, tout, ufull, t_buf,
-         dm_in, dm_out, dv_in, dv_out, c_in, c_out, e_in, e_out, s_buf, b_in, p_out, p_in, ph, pl_,
-         wt_out, wt_in, land, red, red_in, full, lsem, ssem, rsem):
+         dm_in, dm_out, dv_in, dv_out, c_in, c_out, e_in, e_out, s_buf, b_in, p_in, ph, pl_,
+         wt_out, wt_in, land, src, v_parts, s_parts, h_buf, red, red_in, full, lsem, ssem, rsem):
     B = F.shape[1]
     R = V.shape[0]
     M = Y.shape[1]
@@ -148,23 +148,28 @@
 
     for copy in loads[4:6]:
         copy.wait()
-    src_re = jnp.concatenate([mm(F[0, top], y), last_re], axis=0)
-    src_im = jnp.concatenate([mm(F[1, top], y), last_im], axis=0)
-    f_right = jnp.concatenate([F[0, :, last], F[1, :, last]], axis=0)
-    p_rows = mm(f_right, vs[0]) + mm(f_right, vs[1])
-    cde[core, 0] = jnp.concatenate([p_rows[:R].T, p_rows[B : B + R].T], axis=1)
-    cde[core, 1] = jnp.concatenate(
-        [F[0, :R, :R].astype(f32).T, F[1, :R, :R].astype(f32).T], axis=1
-    )
-    cde[core, 2] = jnp.concatenate([src_re[:R].T, src_im[:R].T], axis=1)
+    v_parts[0] = vs[0]
+    v_parts[1] = vs[1]
+
+    @pl.loop(0, 2)
+    def _(part):
+        lanes = pl.ds(pl.multiple_of(part * R, R), R)
+        rows_src = mm(F[part], Y[...])
+        src[part] = rows_src
+        right = F[part, :, last]
+        p_part = mm(right, v_parts[0]) + mm(right, v_parts[1])
+        p_in[0, :, lanes] = p_part
+        cde[core, 0, :, lanes] = p_part[:R].T
+        cde[core, 1, :, lanes] = F[part, :R, :R].astype(f32).T
+        cde[core, 2, :, lanes] = rows_src[:R].T
+
     pair_cde.start()
-    p_out[...] = jnp.concatenate([p_rows[:B], p_rows[B:]], axis=1)
     r_p = [fresh(1) for _ in range(1, nq)]
     r_b = [fresh(1) for _ in range(1, nq)]
     r_wt = [fresh(1) for _ in range(2 * nq)]
     away = lax.rem(q - target + nq, nq)
     slot = jnp.maximum(away - 1, 0)
-    send_p = remote(p_out, p_in.at[slot], r_p[0] + slot, quad=target)
+    send_p = remote(p_in.at[0], p_in.at[slot + 1], r_p[0] + slot, quad=target)
     send_b = remote(s_buf, b_in.at[slot], r_b[0] + slot, quad=target)
 
     @pl.when(q != target)
@@ -328,8 +333,12 @@
     u_left = times(u_chip, e_al) + abs_[0, R:]
     u_own = jnp.where(core == 0, u_chip, u_left)
     wu = split(jnp.concatenate(weighted(u_own), axis=1))
-    f_left = jnp.concatenate([F[0, :, :R], F[1, :, :R]], axis=1)
-    s_buf[...] = wr * src_re - wi * src_im + (nt(f_left, wu[0]) + nt(f_left, wu[1]))
+
+    @pl.loop(0, 2)
+    def _(part):
+        some = pl.ds(pl.multiple_of(part * (B // 2), B // 2), B // 2)
+        f_left = jnp.concatenate([F[0, some, :R], F[1, some, :R]], axis=1)
+        s_buf[some, :] = wr * src[0, some] - wi * src[1, some] + (nt(f_left, wu[0]) + nt(f_left, wu[1]))
 
     @pl.when(q != target)
     def _():
@@ -391,16 +400,20 @@
 
     @pl.when(q == target)
     def _():
-        total = s_buf[...]
         for d in range(1, nq):
             arrival(b_in.at[d - 1], r_b[d - 1]).wait_recv()
-            total += b_in[d - 1]
-        for d in range(nq):
-            if d > 0:
-                arrival(p_in.at[d - 1], r_p[d - 1]).wait_recv()
-            piece = split(p_out[...] if d == 0 else p_in[d - 1])
-            ph[:, d * 2 * R : (d + 1) * 2 * R] = piece[0]
-            pl_[:, d * 2 * R : (d + 1) * 2 * R] = piece[1]
+            arrival(p_in.at[d], r_p[d - 1]).wait_recv()
+
+        @pl.loop(0, nq)
+        def _(d):
+            piece = split(p_in[d])
+            ph[d] = piece[0]
+            pl_[d] = piece[1]
+
+        @pl.loop(0, nq - 1)
+        def _(d):
+            s_buf[...] += b_in[d]
+
         for d in range(nq):
             for k in (0, 1):
                 if d > 0:
@@ -409,9 +422,13 @@
                     @pl.when(core != k)
                     def _():
                         arrival(wt_in.at[0, k * hb : (k + 1) * hb], r_wt[k]).wait_recv()
-        zh, zl = split(jnp.concatenate([wt_in[d] for d in range(nq)], axis=1))
-        total += nt(ph[...], zh) + (nt(ph[...], zl) + nt(pl_[...], zh))
-        s_buf[...] = total
+
+        @pl.loop(0, nq)
+        def _(d):
+            zh, zl = split(wt_in[d])
+            s_buf[...] += nt(ph[d], zh) + (nt(ph[d], zl) + nt(pl_[d], zh))
+
+        total = s_buf[...]
         for p in range(nq):
             @pl.when(q == p)
             def _():
@@ -421,13 +438,20 @@
             def _():
                 shares[p].start()
         ts = split(total)
-        half_h = dot3((onh[...], onl[...]), ts)
+        s_parts[0] = ts[0]
+        s_parts[1] = ts[1]
+
+        @pl.loop(0, 2)
+        def _(part):
+            some = pl.ds(pl.multiple_of(part * (B // 2), B // 2), B // 2)
+            h_buf[some, :] = dot3((onh[some, :], onl[some, :]), (s_parts[0], s_parts[1]))
+
         following = wt_in[0, :, :R]
         for d in range(1, nq):
             following += wt_in[d, :, :R]
         fs = split(following)
         upper = nt(vs[0], fs[0]) + (nt(vs[0], fs[1]) + nt(vs[1], fs[0]))
-        weighted_rows = split(jnp.concatenate([half_h[top], half_h[last] + upper], axis=0))
+        weighted_rows = split(jnp.concatenate([h_buf[top], h_buf[last] + upper], axis=0))
         both = tuple(jnp.concatenate([a, b], axis=1) for a, b in zip(ts, weighted_rows))
         products = dot3(split(total.T), both)
         gram, x = products[:, :M], products[:, M:]
@@ -557,9 +581,10 @@
             thin, thin, thin, thin, wide, thin,
             wide, wide, thin, thin, wide, wide, thin, thin,
             vm((B, M), f32), vm((nq - 1, B, M), f32),
-            vm((B, 2 * R), f32), vm((nq - 1, B, 2 * R), f32),
-            vm((B, 2 * nq * R), bf16), vm((B, 2 * nq * R), bf16),
+            vm((nq, B, 2 * R), f32),
+            vm((nq, B, 2 * R), bf16), vm((nq, B, 2 * R), bf16),
             vm((2, hb, 2 * R), f32), vm((nq, M, 2 * R), f32), vm((qrows, M), f32),
+            vm((2, B, M), f32), vm((2, R, R), bf16), vm((2, B, M), bf16), vm((B, M), f32),
             vm((ns, ch + 8, M), f32), vm((ns - 1, ch + 8, M), f32), vm((ns, ch + 8, M), f32),
             pltpu.SemaphoreType.DMA((7,)),
             pltpu.SemaphoreType.DMA((sends,)),

time: 46.3 us -> 47.1 us (1.017)
  Pallas kernels: 45.5 us -> 46.3 us
    pallas_call x1, Pallas kernels: 43.8 us -> 44.6 us  [per_device(): pl.pallas_call(functools.partial(body, nq, ns), out_shape=(jax.ShapeDtype...]
where the time goes in v4:
time: 47.1 us; the launch traced here: 46.9 us
  Pallas kernels  46.3 us (98%)
  between operations  0.64 us (1%)
    pallas_call x1, Pallas kernels, per_device(): pl.pallas_call(functools.partial(body, nq, ns), out_shape=(jax.ShapeDtype...  44.6 us
    pallas_call x1, Pallas kernels, per_device(): pl.pallas_call(unpack, out_shape=(jax.ShapeDtypeStruct((1, qrows, M), f32...  1.68 us

profile of v4, /device:TPU:0, one launch (start us, length us, event | category | flops | bytes accessed | tf_op | source)
XLA Modules:
  0.0 46.9 jit_solution(7519714805972107199)
XLA Ops:
  0.6 44.6 %shard_map.76 = (f32[1,128,128]{2,1,0:T(8,128)}, f32[136,128]{1,0:T(8,128)}) custom-call(bf16[1,1,2,512,512]{4,3,2,1,0:T(8,128)(2,1)} %f_hbm.1, f32[1,512,512]{2,1,0:T(8,128)} %on_hbm.1, f32[1,128,128]{2,1,0:T(8,128)} %v_hbm.1, bf16[1,512,128]{2,1,0:T(8,128)(2,1)} %y_hbm.1, f32[1,2]{1,0:T(1,128)} %w_ref.1), custom_call_target="tpu_custom_call" | custom-call | tf_op jit(solution)/shard_map/pallas_call | solution.py:569
  45.2 1.7 %shard_map.77 = (f32[1,128,128]{2,1,0:T(8,128)}, f32[128,128]{1,0:T(8,128)}, f32[128,128]{1,0:T(8,128)}) custom-call(f32[1,128,128]{2,1,0:T(8,128)} %get-tuple-element.5.sub_ref, f32[136,128]{1,0:T(8,128)} %get-tuple-element.6.tile_ref), custom_call_target="tpu_custom_call" | custom-call | tf_op jit(solution)/shard_map/pallas_call | solution.py:597

commit v5 on v3

--- a/solution.py
+++ b/solution.py
@@ -158,14 +158,14 @@
     )
     cde[core, 2] = jnp.concatenate([src_re[:R].T, src_im[:R].T], axis=1)
     pair_cde.start()
-    p_out[...] = jnp.concatenate([p_rows[:B], p_rows[B:]], axis=1)
+    p_out[...] = jnp.concatenate([p_rows[R:B], p_rows[B + R :]], axis=1)
     r_p = [fresh(1) for _ in range(1, nq)]
     r_b = [fresh(1) for _ in range(1, nq)]
     r_wt = [fresh(1) for _ in range(2 * nq)]
     away = lax.rem(q - target + nq, nq)
     slot = jnp.maximum(away - 1, 0)
     send_p = remote(p_out, p_in.at[slot], r_p[0] + slot, quad=target)
-    send_b = remote(s_buf, b_in.at[slot], r_b[0] + slot, quad=target)
+    send_b = remote(s_buf.at[R:], b_in.at[slot], r_b[0] + slot, quad=target)
 
     @pl.when(q != target)
     def _():
@@ -328,14 +328,16 @@
     u_left = times(u_chip, e_al) + abs_[0, R:]
     u_own = jnp.where(core == 0, u_chip, u_left)
     wu = split(jnp.concatenate(weighted(u_own), axis=1))
-    f_left = jnp.concatenate([F[0, :, :R], F[1, :, :R]], axis=1)
-    s_buf[...] = wr * src_re - wi * src_im + (nt(f_left, wu[0]) + nt(f_left, wu[1]))
+    f_left = jnp.concatenate([F[0, R:, :R], F[1, R:, :R]], axis=1)
+    s_buf[R:, :] = wr * src_re[R:] - wi * src_im[R:] + (nt(f_left, wu[0]) + nt(f_left, wu[1]))
 
     @pl.when(q != target)
     def _():
         send_b.start()
 
     t_const = times(dot3(us, e_al) + half(abs_[0, R:]), e_dr) + half(er)
+    first_const = dot3(us, e_d) + d_half
+    e_both = tuple(jnp.concatenate([a, b], axis=1) for a, b in zip(e_cr, e_c))
     loads[6].wait()
 
     @pl.when(q == target)
@@ -357,11 +359,13 @@
             t_buf[...] = times(tmid[...], embed(c_in[...])) + e_in[...]
 
     t_in = t_buf[...]
-    wt_out[1] = jnp.concatenate(weighted(t_in), axis=1)
+    t_both = times(t_in, e_both)
+    w_left = weighted(t_both[:, : 2 * R] + t_const)
+    w_first = weighted(t_both[:, 2 * R :] + first_const)
+    wt_out[1] = jnp.concatenate([*weighted(t_in), w_left[0]], axis=1)
+    wt_out[0] = jnp.concatenate([*w_left, w_first[0]], axis=1)
     to_home = []
     for k in (1, 0):
-        if k == 0:
-            wt_out[0] = jnp.concatenate(weighted(times(t_in, e_cr) + t_const), axis=1)
         at = nq // 2 - 1 + k
         hop = lax.rem(q - at + nq, nq)
         mine = jnp.logical_and(q == at, core == k)
@@ -391,7 +395,7 @@
 
     @pl.when(q == target)
     def _():
-        total = s_buf[...]
+        total = s_buf[R:, :]
         for d in range(1, nq):
             arrival(b_in.at[d - 1], r_b[d - 1]).wait_recv()
             total += b_in[d - 1]
@@ -409,8 +413,12 @@
                     @pl.when(core != k)
                     def _():
                         arrival(wt_in.at[0, k * hb : (k + 1) * hb], r_wt[k]).wait_recv()
-        zh, zl = split(jnp.concatenate([wt_in[d] for d in range(nq)], axis=1))
+        zh, zl = split(jnp.concatenate([wt_in[d, :, : 2 * R] for d in range(nq)], axis=1))
         total += nt(ph[...], zh) + (nt(ph[...], zl) + nt(pl_[...], zh))
+        first = wt_in[0, :, 2 * R :]
+        for d in range(1, nq):
+            first += wt_in[d, :, 2 * R :]
+        total = jnp.concatenate([first.T, total], axis=0)
         s_buf[...] = total
         for p in range(nq):
             @pl.when(q == p)
@@ -556,10 +564,10 @@
             vm((2, R + M, 2 * R), f32), vm((2, 3, R, 2 * R), f32),
             thin, thin, thin, thin, wide, thin,
             wide, wide, thin, thin, wide, wide, thin, thin,
-            vm((B, M), f32), vm((nq - 1, B, M), f32),
-            vm((B, 2 * R), f32), vm((nq - 1, B, 2 * R), f32),
-            vm((B, 2 * nq * R), bf16), vm((B, 2 * nq * R), bf16),
-            vm((2, hb, 2 * R), f32), vm((nq, M, 2 * R), f32), vm((qrows, M), f32),
+            vm((B, M), f32), vm((nq - 1, B - R, M), f32),
+            vm((B - R, 2 * R), f32), vm((nq - 1, B - R, 2 * R), f32),
+            vm((B - R, 2 * nq * R), bf16), vm((B - R, 2 * nq * R), bf16),
+            vm((2, hb, 3 * R), f32), vm((nq, M, 3 * R), f32), vm((qrows, M), f32),
             vm((ns, ch + 8, M), f32), vm((ns - 1, ch + 8, M), f32), vm((ns, ch + 8, M), f32),
             pltpu.SemaphoreType.DMA((7,)),
             pltpu.SemaphoreType.DMA((sends,)),

time: 46.3 us -> 45.9 us (level)
  no operation moved by 1% of the time
where the time goes in v5:
time: 45.9 us; the launch traced here: 45.7 us
  Pallas kernels  45.1 us (98%)
  between operations  0.64 us (1%)
    pallas_call x1, Pallas kernels, per_device(): pl.pallas_call(functools.partial(body, nq, ns), out_shape=(jax.ShapeDtype...  43.4 us
    pallas_call x1, Pallas kernels, per_device(): pl.pallas_call(unpack, out_shape=(jax.ShapeDtypeStruct((1, qrows, M), f32...  1.68 us

profile of v5, /device:TPU:0, one launch (start us, length us, event | category | flops | bytes accessed | tf_op | source)
XLA Modules:
  0.0 45.7 jit_solution(2369973482535603382)
XLA Ops:
  0.6 43.4 %shard_map.76 = (f32[1,128,128]{2,1,0:T(8,128)}, f32[136,128]{1,0:T(8,128)}) custom-call(bf16[1,1,2,512,512]{4,3,2,1,0:T(8,128)(2,1)} %f_hbm.1, f32[1,512,512]{2,1,0:T(8,128)} %on_hbm.1, f32[1,128,128]{2,1,0:T(8,128)} %v_hbm.1, bf16[1,512,128]{2,1,0:T(8,128)(2,1)} %y_hbm.1, f32[1,2]{1,0:T(1,128)} %w_ref.1), custom_call_target="tpu_custom_call" | custom-call | tf_op jit(solution)/shard_map/pallas_call | solution.py:553
  44.1 1.7 %shard_map.77 = (f32[1,128,128]{2,1,0:T(8,128)}, f32[128,128]{1,0:T(8,128)}, f32[128,128]{1,0:T(8,128)}) custom-call(f32[1,128,128]{2,1,0:T(8,128)} %get-tuple-element.5.sub_ref, f32[136,128]{1,0:T(8,128)} %get-tuple-element.6.tile_ref), custom_call_target="tpu_custom_call" | custom-call | tf_op jit(solution)/shard_map/pallas_call | solution.py:580

commit v6 on v5

--- a/solution.py
+++ b/solution.py
@@ -151,14 +151,14 @@
     src_re = jnp.concatenate([mm(F[0, top], y), last_re], axis=0)
     src_im = jnp.concatenate([mm(F[1, top], y), last_im], axis=0)
     f_right = jnp.concatenate([F[0, :, last], F[1, :, last]], axis=0)
-    p_rows = mm(f_right, vs[0]) + mm(f_right, vs[1])
-    cde[core, 0] = jnp.concatenate([p_rows[:R].T, p_rows[B : B + R].T], axis=1)
+    p_flat = nt(vts[0], f_right) + nt(vts[1], f_right)
+    cde[core, 0] = jnp.concatenate([p_flat[:, :R], p_flat[:, B : B + R]], axis=1)
     cde[core, 1] = jnp.concatenate(
         [F[0, :R, :R].astype(f32).T, F[1, :R, :R].astype(f32).T], axis=1
     )
     cde[core, 2] = jnp.concatenate([src_re[:R].T, src_im[:R].T], axis=1)
     pair_cde.start()
-    p_out[...] = jnp.concatenate([p_rows[R:B], p_rows[B + R :]], axis=1)
+    p_out[...] = jnp.concatenate([p_flat[:, R:B], p_flat[:, B + R :]], axis=0)
     r_p = [fresh(1) for _ in range(1, nq)]
     r_b = [fresh(1) for _ in range(1, nq)]
     r_wt = [fresh(1) for _ in range(2 * nq)]
@@ -346,17 +346,16 @@
         onh[...] = on[0]
         onl[...] = on[1]
 
-    @pl.when(chip < mid)
+    @pl.when(chip == mid - 1)
     def _():
         back[0].wait_recv()
-
-        @pl.when(chip == mid - 1)
-        def _():
-            t_buf[...] = tmid[...]
-
-        @pl.when(chip < mid - 1)
-        def _():
-            t_buf[...] = times(tmid[...], embed(c_in[...])) + e_in[...]
+        t_buf[...] = tmid[...]
+
+    @pl.when(chip < mid - 1)
+    def _():
+        e_cin = embed(c_in[...])
+        back[0].wait_recv()
+        t_buf[...] = times(tmid[...], e_cin) + e_in[...]
 
     t_in = t_buf[...]
     t_both = times(t_in, e_both)
@@ -399,12 +398,13 @@
         for d in range(1, nq):
             arrival(b_in.at[d - 1], r_b[d - 1]).wait_recv()
             total += b_in[d - 1]
+        total = total.T
         for d in range(nq):
             if d > 0:
                 arrival(p_in.at[d - 1], r_p[d - 1]).wait_recv()
             piece = split(p_out[...] if d == 0 else p_in[d - 1])
-            ph[:, d * 2 * R : (d + 1) * 2 * R] = piece[0]
-            pl_[:, d * 2 * R : (d + 1) * 2 * R] = piece[1]
+            ph[d * 2 * R : (d + 1) * 2 * R] = piece[0]
+            pl_[d * 2 * R : (d + 1) * 2 * R] = piece[1]
         for d in range(nq):
             for k in (0, 1):
                 if d > 0:
@@ -414,11 +414,14 @@
                     def _():
                         arrival(wt_in.at[0, k * hb : (k + 1) * hb], r_wt[k]).wait_recv()
         zh, zl = split(jnp.concatenate([wt_in[d, :, : 2 * R] for d in range(nq)], axis=1))
-        total += nt(ph[...], zh) + (nt(ph[...], zl) + nt(pl_[...], zh))
+        total += mm(zh, ph[...]) + (mm(zl, ph[...]) + mm(zh, pl_[...]))
         first = wt_in[0, :, 2 * R :]
         for d in range(1, nq):
             first += wt_in[d, :, 2 * R :]
-        total = jnp.concatenate([first.T, total], axis=0)
+        flipped = jnp.concatenate([first, total], axis=1)
+        fs = split(flipped)
+        half_h = dot3(fs, (onh[...], onl[...]))
+        total = flipped.T
         s_buf[...] = total
         for p in range(nq):
             @pl.when(q == p)
@@ -429,16 +432,14 @@
             def _():
                 shares[p].start()
         ts = split(total)
-        half_h = dot3((onh[...], onl[...]), ts)
         following = wt_in[0, :, :R]
         for d in range(1, nq):
             following += wt_in[d, :, :R]
-        fs = split(following)
-        upper = nt(vs[0], fs[0]) + (nt(vs[0], fs[1]) + nt(vs[1], fs[0]))
-        weighted_rows = split(jnp.concatenate([half_h[top], half_h[last] + upper], axis=0))
-        both = tuple(jnp.concatenate([a, b], axis=1) for a, b in zip(ts, weighted_rows))
-        products = dot3(split(total.T), both)
-        gram, x = products[:, :M], products[:, M:]
+        upper = dot3(split(following), vts)
+        weighted_rows = split(jnp.concatenate([half_h[:, top], half_h[:, last] + upper], axis=1))
+        both = tuple(jnp.concatenate([a, b], axis=0) for a, b in zip(fs, weighted_rows))
+        products = dot3(both, ts)
+        gram, x = products[:M], products[M:]
         proj = x + x.T
 
         at_row = lax.broadcasted_iota(jnp.int32, (M, M), 0)
@@ -565,8 +566,8 @@
             thin, thin, thin, thin, wide, thin,
             wide, wide, thin, thin, wide, wide, thin, thin,
             vm((B, M), f32), vm((nq - 1, B - R, M), f32),
-            vm((B - R, 2 * R), f32), vm((nq - 1, B - R, 2 * R), f32),
-            vm((B - R, 2 * nq * R), bf16), vm((B - R, 2 * nq * R), bf16),
+            vm((2 * R, B - R), f32), vm((nq - 1, 2 * R, B - R), f32),
+            vm((2 * nq * R, B - R), bf16), vm((2 * nq * R, B - R), bf16),
             vm((2, hb, 3 * R), f32), vm((nq, M, 3 * R), f32), vm((qrows, M), f32),
             vm((ns, ch + 8, M), f32), vm((ns - 1, ch + 8, M), f32), vm((ns, ch + 8, M), f32),
             pltpu.SemaphoreType.DMA((7,)),

time: 45.9 us -> 46 us (level)
  no operation moved by 1% of the time
where the time goes in v6:
time: 46 us; the launch traced here: 45.8 us
  Pallas kernels  45.2 us (98%)
  between operations  0.64 us (1%)
    pallas_call x1, Pallas kernels, per_device(): pl.pallas_call(functools.partial(body, nq, ns), out_shape=(jax.ShapeDtype...  43.5 us
    pallas_call x1, Pallas kernels, per_device(): pl.pallas_call(unpack, out_shape=(jax.ShapeDtypeStruct((1, qrows, M), f32...  1.68 us

profile of v6, /device:TPU:0, one launch (start us, length us, event | category | flops | bytes accessed | tf_op | source)
XLA Modules:
  0.0 45.8 jit_solution(10254791838386943737)
XLA Ops:
  0.6 43.5 %shard_map.76 = (f32[1,128,128]{2,1,0:T(8,128)}, f32[136,128]{1,0:T(8,128)}) custom-call(bf16[1,1,2,512,512]{4,3,2,1,0:T(8,128)(2,1)} %f_hbm.1, f32[1,512,512]{2,1,0:T(8,128)} %on_hbm.1, f32[1,128,128]{2,1,0:T(8,128)} %v_hbm.1, bf16[1,512,128]{2,1,0:T(8,128)(2,1)} %y_hbm.1, f32[1,2]{1,0:T(1,128)} %w_ref.1), custom_call_target="tpu_custom_call" | custom-call | tf_op jit(solution)/shard_map/pallas_call | solution.py:554
  44.1 1.7 %shard_map.77 = (f32[1,128,128]{2,1,0:T(8,128)}, f32[128,128]{1,0:T(8,128)}, f32[128,128]{1,0:T(8,128)}) custom-call(f32[1,128,128]{2,1,0:T(8,128)} %get-tuple-element.5.sub_ref, f32[136,128]{1,0:T(8,128)} %get-tuple-element.6.tile_ref), custom_call_target="tpu_custom_call" | custom-call | tf_op jit(solution)/shard_map/pallas_call | solution.py:581

commit v7 on v6

--- a/solution.py
+++ b/solution.py
@@ -53,7 +53,7 @@
 def body(nq, ns, f_hbm, on_hbm, v_hbm, y_hbm, w_ref, sub_ref, tile_ref,
          F, ON, V, Y, onh, onl, abs_, cde, uin, uout, tmid, tout, ufull, t_buf,
          dm_in, dm_out, dv_in, dv_out, c_in, c_out, e_in, e_out, s_buf, b_in, p_out, p_in, ph, pl_,
-         wt_out, wt_in, land, red, red_in, full, lsem, ssem, rsem):
+         wt_out, wt_in, land, red, red_in, full, lsem, ssem, rsem, bsem):
     B = F.shape[1]
     R = V.shape[0]
     M = Y.shape[1]
@@ -86,18 +86,15 @@
         copy.start()
 
     barrier = pltpu.get_barrier_semaphore()
-    for d in range(1, ns):
-        pl.semaphore_signal(barrier, inc=1, device_id={"slab": lax.rem(s + d, ns)}, device_id_type=MESH)
-    for d in range(1, nq):
-        pl.semaphore_signal(barrier, inc=1, device_id={"quad": lax.rem(q + d, nq)}, device_id_type=MESH)
-        pl.semaphore_signal(
-            barrier, inc=1, device_id={"quad": lax.rem(q + d, nq), "slab": buddy}, device_id_type=MESH)
-
-    @pl.when(q == target)
-    def _():
-        for d in range(2, ns, 2):
-            to = lax.rem(buddy + d, ns)
-            pl.semaphore_signal(barrier, inc=1, device_id={"quad": home(to), "slab": to}, device_id_type=MESH)
+    others = ns * nq - 1
+
+    def peer(i):
+        to = lax.rem(q * ns + s + 1 + i, ns * nq)
+        return {"quad": to // ns, "slab": lax.rem(to, ns)}
+
+    @pl.loop(0, others)
+    def _(i):
+        pl.semaphore_signal(barrier, inc=1, device_id=peer(i), device_id_type=MESH)
 
     counts = [0, 0]
 
@@ -131,15 +128,7 @@
     abs_[core, :R] = jnp.concatenate([a_cols[:, :R].T, a_cols[:, R:].T], axis=1)
     abs_[core, R:] = jnp.concatenate([b_cols[:, :M].T, b_cols[:, M:].T], axis=1)
 
-    base_wait = ns - 1 + 2 * (nq - 1)
-
-    @pl.when(q == target)
-    def _():
-        pl.semaphore_wait(barrier, base_wait + ns // 2 - 1)
-
-    @pl.when(q != target)
-    def _():
-        pl.semaphore_wait(barrier, base_wait)
+    pl.semaphore_wait(barrier, others)
 
     r_ab, r_cde = fresh(1), fresh(1)
     pair_ab = remote(abs_.at[core], abs_.at[core], r_ab, slab=buddy)
@@ -177,13 +166,12 @@
     def half(x):
         return jnp.where(core == 0, x[:hb], x[hb:])
 
-    r_u, r_t, r_dm, r_dv, r_relay, r_c, r_e = (fresh(1) for _ in range(7))
+    r_u, r_t, r_dm, r_dv, r_c, r_e = (fresh(1) for _ in range(6))
     left = jnp.maximum(s - 2, core)
     forward = remote(uout, uin, r_u, slab=jnp.minimum(s + 2, ns - 2 + core))
     back = [remote(tout, tmid, r_t, slab=2 * c + core) for c in range(mid)]
-    send_dm = remote(dm_out.at[rows], dm_in.at[rows], r_dm, slab=left)
+    send_dm = remote(dm_out, dm_in, r_dm, slab=left)
     send_dv = remote(dv_out, dv_in, r_dv, slab=left)
-    relay = remote(dm_in.at[rows], dm_in.at[rows], r_relay, slab=buddy)
     send_c = remote(c_out, c_in, r_c, slab=left)
     send_e = remote(e_out, e_in, r_e, slab=left)
     inner_left = jnp.logical_and(chip > 0, chip < mid)
@@ -220,12 +208,9 @@
 
     @pl.when(jnp.logical_and(chip >= mid, chip < nc - 1))
     def _():
-        send_dm.wait_recv()
-        relay.start()
-
         @pl.when(chip > mid)
         def _():
-            arrival(dm_in.at[other_rows], r_relay).wait_recv()
+            send_dm.wait_recv()
             z = times(jnp.concatenate([ab[:R], b_half], axis=0), embed(dm_in[...]))
             send_dv.wait_recv()
             z_b = z[R:] + dv_in[...]
@@ -278,7 +263,7 @@
 
             @pl.when(chip == mid)
             def _():
-                arrival(dm_in.at[other_rows], r_relay).wait_recv()
+                send_dm.wait_recv()
                 send_dv.wait_recv()
 
             t_in = times(u_out, embed(dm_in[...])) + dv_in[...]
@@ -380,7 +365,8 @@
         def _():
             copy.start()
 
-    r_sub, r_line = fresh(1), fresh(1)
+    r_sub = fresh(1)
+    r_full = [fresh(1) for _ in range(ns)]
     shares = [
         remote(s_buf.at[slice(p * qrows, (p + 1) * qrows)], land, r_sub, quad=p)
         for p in range(nq)
@@ -390,7 +376,12 @@
     for d in range(1, ns):
         to = lax.rem(s + d, ns)
         scatter.append(remote(red.at[to], red_in.at[d - 1], r_red[d - 1], quad=home(to), slab=to))
-    line = [remote(full.at[s], full.at[s], r_line, quad=lax.rem(q + d, nq)) for d in range(1, nq)]
+
+    def whole(i):
+        return pltpu.make_async_remote_copy(
+            src_ref=full.at[s], dst_ref=full.at[s], send_sem=bsem.at[i],
+            recv_sem=rsem.at[r_full[0] + s], device_id=peer(i), device_id_type=MESH,
+        )
 
     @pl.when(q == target)
     def _():
@@ -457,29 +448,26 @@
             scatter[d - 1].wait_recv()
             part += red_in[d - 1]
         full[s] = part
-        for copy in line:
-            copy.start()
+
+        @pl.loop(0, others)
+        def _(i):
+            whole(i).start()
 
     @pl.when(q != target)
     def _():
-        arrival(full.at[s], r_line).wait_recv()
         shares[0].wait_recv()
 
-    spread, r_spread = [], []
-    for d in range(1, ns):
-        r_spread.append(fresh(1))
-        copy = remote(full.at[s], full.at[s], r_spread[-1], slab=lax.rem(s + d, ns))
-        copy.start()
-        spread.append(copy)
     sub_ref[0] = land[...]
-    for d in range(1, ns):
-        arrival(full.at[lax.rem(s - d + ns, ns)], r_spread[d - 1]).wait_recv()
+    for i in range(ns):
+        @pl.when(jnp.logical_or(q != target, s != i))
+        def _():
+            arrival(full.at[i], r_full[i]).wait_recv()
     scale = 1.0 / (ns * B)
     for i in range(ns):
         tile_ref[i * ch : (i + 1) * ch, :] = full[i, :ch] * scale
     tile_ref[M : M + 8, :] = full[0, ch : ch + 8] * scale
 
-    for copy in [pair_ab, pair_cde, cross_u] + spread:
+    for copy in [pair_ab, pair_cde, cross_u]:
         copy.wait_send()
 
     @pl.when(chip < nc - 1)
@@ -491,10 +479,6 @@
         send_dm.wait_send()
         send_dv.wait_send()
 
-    @pl.when(jnp.logical_and(chip >= mid, chip < nc - 1))
-    def _():
-        relay.wait_send()
-
     @pl.when(inner_left)
     def _():
         send_c.wait_send()
@@ -517,8 +501,12 @@
 
     @pl.when(q == target)
     def _():
-        for copy in scatter + line:
+        for copy in scatter:
             copy.wait_send()
+
+        @pl.loop(0, others)
+        def _(i):
+            whole(i).wait_send()
 
         for p in range(nq):
             @pl.when(q != p)
@@ -544,8 +532,8 @@
     R = coupling.shape[1]
     M = vectors.shape[2]
     hb, ch, qrows = M // 2, M // ns, B // nq
-    sends = 13 + ns // 4 + nq + 2 * (ns - 1) + (nq - 1)
-    recvs = 12 + 2 * (nq - 1) + 2 * nq + 2 * (ns - 1)
+    sends = 12 + ns // 4 + nq + (ns - 1)
+    recvs = 10 + 2 * (nq - 1) + 2 * nq + (ns - 1) + ns
     vm = pltpu.VMEM
     in_hbm = pl.BlockSpec(memory_space=pltpu.HBM)
     here = pl.BlockSpec(memory_space=pltpu.VMEM)
@@ -573,6 +561,7 @@
             pltpu.SemaphoreType.DMA((7,)),
             pltpu.SemaphoreType.DMA((sends,)),
             pltpu.SemaphoreType.DMA((recvs,)),
+            pltpu.SemaphoreType.DMA((ns * nq,)),
         ],
         compiler_params=pltpu.CompilerParams(
             collective_id=0, has_side_effects=True, vmem_limit_bytes=VMEM_BYTES

time: 46 us -> 45.9 us (level)
  no operation moved by 1% of the time
where the time goes in v7:
time: 45.9 us; the launch traced here: 45.7 us
  Pallas kernels  45.1 us (98%)
  between operations  0.64 us (1%)
    pallas_call x1, Pallas kernels, per_device(): pl.pallas_call(functools.partial(body, nq, ns), out_shape=(jax.ShapeDtype...  43.4 us
    pallas_call x1, Pallas kernels, per_device(): pl.pallas_call(unpack, out_shape=(jax.ShapeDtypeStruct((1, qrows, M), f32...  1.68 us

profile of v7, /device:TPU:0, one launch (start us, length us, event | category | flops | bytes accessed | tf_op | source)
XLA Modules:
  0.0 45.7 jit_solution(9716745012639962443)
XLA Ops:
  0.6 43.4 %shard_map.76 = (f32[1,128,128]{2,1,0:T(8,128)}, f32[136,128]{1,0:T(8,128)}) custom-call(bf16[1,1,2,512,512]{4,3,2,1,0:T(8,128)(2,1)} %f_hbm.1, f32[1,512,512]{2,1,0:T(8,128)} %on_hbm.1, f32[1,128,128]{2,1,0:T(8,128)} %v_hbm.1, bf16[1,512,128]{2,1,0:T(8,128)(2,1)} %y_hbm.1, f32[1,2]{1,0:T(1,128)} %w_ref.1), custom_call_target="tpu_custom_call" | custom-call | tf_op jit(solution)/shard_map/pallas_call | solution.py:542
  44.0 1.7 %shard_map.77 = (f32[1,128,128]{2,1,0:T(8,128)}, f32[128,128]{1,0:T(8,128)}, f32[128,128]{1,0:T(8,128)}) custom-call(f32[1,128,128]{2,1,0:T(8,128)} %get-tuple-element.5.sub_ref, f32[136,128]{1,0:T(8,128)} %get-tuple-element.6.tile_ref), custom_call_target="tpu_custom_call" | custom-call | tf_op jit(solution)/shard_map/pallas_call | solution.py:570

commit v8 on v7

--- a/solution.py
+++ b/solution.py
@@ -156,9 +156,10 @@
     send_p = remote(p_out, p_in.at[slot], r_p[0] + slot, quad=target)
     send_b = remote(s_buf.at[R:], b_in.at[slot], r_b[0] + slot, quad=target)
 
-    @pl.when(q != target)
-    def _():
-        send_p.start()
+    def start_p():
+        @pl.when(q != target)
+        def _():
+            send_p.start()
 
     rows = pl.ds(pl.multiple_of(core * hb, hb), hb)
     other_rows = pl.ds(pl.multiple_of((1 - core) * hb, hb), hb)
@@ -186,6 +187,7 @@
         uin[...] = jnp.zeros_like(uin)
         uout[...] = half(ab[R:])
         forward.start()
+        start_p()
 
     arrival(cde.at[1 - core], r_cde).wait_recv()
     cl, dl, el = cde[0, 0], cde[0, 1], cde[0, 2]
@@ -205,6 +207,7 @@
         dv_out[...] = d_half
         send_dm.start()
         send_dv.start()
+        start_p()
 
     @pl.when(jnp.logical_and(chip >= mid, chip < nc - 1))
     def _():
@@ -274,6 +277,8 @@
                 tout[...] = times(t_in, e_c) + const
                 for copy in back:
                     copy.start()
+
+        start_p()
 
     r_cu = fresh(1)
     ufull[rows, :] = u_in

time: 45.9 us -> 50.3 us (1.096)
  Pallas kernels: 45.1 us -> 49.5 us
    pallas_call x1, Pallas kernels: 43.4 us -> 47.8 us  [per_device(): pl.pallas_call(functools.partial(body, nq, ns), out_shape=(jax.ShapeDtype...]
where the time goes in v8:
time: 50.3 us; the launch traced here: 50.1 us
  Pallas kernels  49.5 us (98%)
  between operations  0.64 us (1%)
    pallas_call x1, Pallas kernels, per_device(): pl.pallas_call(functools.partial(body, nq, ns), out_shape=(jax.ShapeDtype...  47.8 us
    pallas_call x1, Pallas kernels, per_device(): pl.pallas_call(unpack, out_shape=(jax.ShapeDtypeStruct((1, qrows, M), f32...  1.68 us

profile of v8, /device:TPU:0, one launch (start us, length us, event | category | flops | bytes accessed | tf_op | source)
XLA Modules:
  0.0 50.1 jit_solution(15335781812555179867)
XLA Ops:
  0.6 47.8 %shard_map.76 = (f32[1,128,128]{2,1,0:T(8,128)}, f32[136,128]{1,0:T(8,128)}) custom-call(bf16[1,1,2,512,512]{4,3,2,1,0:T(8,128)(2,1)} %f_hbm.1, f32[1,512,512]{2,1,0:T(8,128)} %on_hbm.1, f32[1,128,128]{2,1,0:T(8,128)} %v_hbm.1, bf16[1,512,128]{2,1,0:T(8,128)(2,1)} %y_hbm.1, f32[1,2]{1,0:T(1,128)} %w_ref.1), custom_call_target="tpu_custom_call" | custom-call | tf_op jit(solution)/shard_map/pallas_call | solution.py:547
  48.5 1.7 %shard_map.77 = (f32[1,128,128]{2,1,0:T(8,128)}, f32[128,128]{1,0:T(8,128)}, f32[128,128]{1,0:T(8,128)}) custom-call(f32[1,128,128]{2,1,0:T(8,128)} %get-tuple-element.5.sub_ref, f32[136,128]{1,0:T(8,128)} %get-tuple-element.6.tile_ref), custom_call_target="tpu_custom_call" | custom-call | tf_op jit(solution)/shard_map/pallas_call | solution.py:575

commit v9 on v7

--- a/solution.py
+++ b/solution.py
@@ -169,6 +169,8 @@
     r_u, r_t, r_dm, r_dv, r_c, r_e = (fresh(1) for _ in range(6))
     left = jnp.maximum(s - 2, core)
     forward = remote(uout, uin, r_u, slab=jnp.minimum(s + 2, ns - 2 + core))
+    r_cu = fresh(1)
+    cross_u = remote(uout, ufull.at[rows], r_cu, slab=jnp.minimum(s + 2, ns - 2 + core) + 1 - 2 * core)
     back = [remote(tout, tmid, r_t, slab=2 * c + core) for c in range(mid)]
     send_dm = remote(dm_out, dm_in, r_dm, slab=left)
     send_dv = remote(dv_out, dv_in, r_dv, slab=left)
@@ -184,8 +186,10 @@
     @pl.when(chip == 0)
     def _():
         uin[...] = jnp.zeros_like(uin)
+        ufull[...] = jnp.zeros_like(ufull)
         uout[...] = half(ab[R:])
         forward.start()
+        cross_u.start()
 
     arrival(cde.at[1 - core], r_cde).wait_recv()
     cl, dl, el = cde[0, 0], cde[0, 1], cde[0, 2]
@@ -256,6 +260,7 @@
         u_out = dot3(us, e_out_map) + b_half
         uout[...] = u_out
         forward.start()
+        cross_u.start()
 
         @pl.when(chip >= mid)
         def _():
@@ -275,10 +280,7 @@
                 for copy in back:
                     copy.start()
 
-    r_cu = fresh(1)
     ufull[rows, :] = u_in
-    cross_u = remote(ufull.at[rows], ufull.at[rows], r_cu, slab=buddy)
-    cross_u.start()
 
     @pl.when(inner_left)
     def _():
@@ -306,7 +308,10 @@
         re, im = x[:, :R], x[:, R:]
         return wr * re - wi * im, -(wr * im + wi * re)
 
-    arrival(ufull.at[other_rows], r_cu).wait_recv()
+    @pl.when(chip > 0)
+    def _():
+        arrival(ufull.at[other_rows], r_cu).wait_recv()
+
     u_chip = ufull[...]
     e_al = embed(abs_[0, :R])
     e_cr = embed(cr)
@@ -467,12 +472,13 @@
         tile_ref[i * ch : (i + 1) * ch, :] = full[i, :ch] * scale
     tile_ref[M : M + 8, :] = full[0, ch : ch + 8] * scale
 
-    for copy in [pair_ab, pair_cde, cross_u]:
+    for copy in [pair_ab, pair_cde]:
         copy.wait_send()
 
     @pl.when(chip < nc - 1)
     def _():
         forward.wait_send()
+        cross_u.wait_send()
 
     @pl.when(chip > mid)
     def _():

time: 45.9 us -> 45.4 us (0.989)
  Pallas kernels: 45.1 us -> 44.6 us
    pallas_call x1, Pallas kernels: 43.4 us -> 42.9 us  [per_device(): pl.pallas_call(functools.partial(body, nq, ns), out_shape=(jax.ShapeDtype...]
where the time goes in v9:
time: 45.4 us; the launch traced here: 45.2 us
  Pallas kernels  44.6 us (98%)
  between operations  0.64 us (1%)
    pallas_call x1, Pallas kernels, per_device(): pl.pallas_call(functools.partial(body, nq, ns), out_shape=(jax.ShapeDtype...  42.9 us
    pallas_call x1, Pallas kernels, per_device(): pl.pallas_call(unpack, out_shape=(jax.ShapeDtypeStruct((1, qrows, M), f32...  1.68 us

profile of v9, /device:TPU:0, one launch (start us, length us, event | category | flops | bytes accessed | tf_op | source)
XLA Modules:
  0.0 45.2 jit_solution(4629421892154342206)
XLA Ops:
  0.6 42.9 %shard_map.76 = (f32[1,128,128]{2,1,0:T(8,128)}, f32[136,128]{1,0:T(8,128)}) custom-call(bf16[1,1,2,512,512]{4,3,2,1,0:T(8,128)(2,1)} %f_hbm.1, f32[1,512,512]{2,1,0:T(8,128)} %on_hbm.1, f32[1,128,128]{2,1,0:T(8,128)} %v_hbm.1, bf16[1,512,128]{2,1,0:T(8,128)(2,1)} %y_hbm.1, f32[1,2]{1,0:T(1,128)} %w_ref.1), custom_call_target="tpu_custom_call" | custom-call | tf_op jit(solution)/shard_map/pallas_call | solution.py:548
  43.5 1.7 %shard_map.77 = (f32[1,128,128]{2,1,0:T(8,128)}, f32[128,128]{1,0:T(8,128)}, f32[128,128]{1,0:T(8,128)}) custom-call(f32[1,128,128]{2,1,0:T(8,128)} %get-tuple-element.5.sub_ref, f32[136,128]{1,0:T(8,128)} %get-tuple-element.6.tile_ref), custom_call_target="tpu_custom_call" | custom-call | tf_op jit(solution)/shard_map/pallas_call | solution.py:576

commit v10 on v9

--- a/solution.py
+++ b/solution.py
@@ -141,12 +141,6 @@
     src_im = jnp.concatenate([mm(F[1, top], y), last_im], axis=0)
     f_right = jnp.concatenate([F[0, :, last], F[1, :, last]], axis=0)
     p_flat = nt(vts[0], f_right) + nt(vts[1], f_right)
-    cde[core, 0] = jnp.concatenate([p_flat[:, :R], p_flat[:, B : B + R]], axis=1)
-    cde[core, 1] = jnp.concatenate(
-        [F[0, :R, :R].astype(f32).T, F[1, :R, :R].astype(f32).T], axis=1
-    )
-    cde[core, 2] = jnp.concatenate([src_re[:R].T, src_im[:R].T], axis=1)
-    pair_cde.start()
     p_out[...] = jnp.concatenate([p_flat[:, R:B], p_flat[:, B + R :]], axis=0)
     r_p = [fresh(1) for _ in range(1, nq)]
     r_b = [fresh(1) for _ in range(1, nq)]
@@ -159,6 +153,13 @@
     @pl.when(q != target)
     def _():
         send_p.start()
+
+    cde[core, 0] = jnp.concatenate([p_flat[:, :R], p_flat[:, B : B + R]], axis=1)
+    cde[core, 1] = jnp.concatenate(
+        [F[0, :R, :R].astype(f32).T, F[1, :R, :R].astype(f32).T], axis=1
+    )
+    cde[core, 2] = jnp.concatenate([src_re[:R].T, src_im[:R].T], axis=1)
+    pair_cde.start()
 
     rows = pl.ds(pl.multiple_of(core * hb, hb), hb)
     other_rows = pl.ds(pl.multiple_of((1 - core) * hb, hb), hb)

time: 45.4 us -> 45.4 us (level)
  no operation moved by 1% of the time
where the time goes in v10:
time: 45.4 us; the launch traced here: 45.2 us
  Pallas kernels  44.6 us (98%)
  between operations  0.64 us (1%)
    pallas_call x1, Pallas kernels, per_device(): pl.pallas_call(functools.partial(body, nq, ns), out_shape=(jax.ShapeDtype...  42.9 us
    pallas_call x1, Pallas kernels, per_device(): pl.pallas_call(unpack, out_shape=(jax.ShapeDtypeStruct((1, qrows, M), f32...  1.68 us

profile of v10, /device:TPU:0, one launch (start us, length us, event | category | flops | bytes accessed | tf_op | source)
XLA Modules:
  0.0 45.2 jit_solution(11668859077731892925)
XLA Ops:
  0.6 42.9 %shard_map.76 = (f32[1,128,128]{2,1,0:T(8,128)}, f32[136,128]{1,0:T(8,128)}) custom-call(bf16[1,1,2,512,512]{4,3,2,1,0:T(8,128)(2,1)} %f_hbm.1, f32[1,512,512]{2,1,0:T(8,128)} %on_hbm.1, f32[1,128,128]{2,1,0:T(8,128)} %v_hbm.1, bf16[1,512,128]{2,1,0:T(8,128)(2,1)} %y_hbm.1, f32[1,2]{1,0:T(1,128)} %w_ref.1), custom_call_target="tpu_custom_call" | custom-call | tf_op jit(solution)/shard_map/pallas_call | solution.py:549
  43.6 1.7 %shard_map.77 = (f32[1,128,128]{2,1,0:T(8,128)}, f32[128,128]{1,0:T(8,128)}, f32[128,128]{1,0:T(8,128)}) custom-call(f32[1,128,128]{2,1,0:T(8,128)} %get-tuple-element.5.sub_ref, f32[136,128]{1,0:T(8,128)} %get-tuple-element.6.tile_ref), custom_call_target="tpu_custom_call" | custom-call | tf_op jit(solution)/shard_map/pallas_call | solution.py:577
